TPU v7x, 256 devices: a whole 4x4x8 slice. The times are simulated.
256 devices in a mesh: dom: 64 (over y, z_hi, x), gp: 4 (over z_lo, core).
Axes of the slice: x: 4, y: 4, z: 8 (z_hi: 4, z_lo: 2; z = z_hi * 2 + z_lo), core: 2. Of those that a mesh axis runs over, the one named last changes fastest.
Arguments:
- atoms: bfloat16 [65536, 512], P(('dom', 'gp')), may hold values from -6 to 6
- messages: bfloat16 [524288, 512], P(('dom', 'gp')), may hold values from -6 to 6
- edge_src: int32 [524288], P(('dom', 'gp')), may hold values from 0 to 2047
- edge_dst: int32 [524288], P(('dom', 'gp')), may hold values from 0 to 1023
- trip_in: int32 [524288], P(('dom', 'gp')), may hold values from 0 to 2047
- trip_out: int32 [524288], P(('dom', 'gp')), may hold values from 0 to 2047
- trip_basis: bfloat16 [524288, 64], P(('dom', 'gp')), may hold values from -6 to 6
- edge_count: int32 [256], P(('dom', 'gp')), may hold values from 256 to 2048, as said below
- trip_count: int32 [256], P(('dom', 'gp')), may hold values from 256 to 2048, as said below
- w_a: bfloat16 [512, 512], replicated, may hold values from -0.25 to 0.25
- w_down: bfloat16 [512, 64], replicated, may hold values from -0.25 to 0.25
- w_t: bfloat16 [64, 512], replicated, may hold values from -0.75 to 0.75
- w_b: bfloat16 [512, 512], replicated, may hold values from -0.25 to 0.25
- cotangent: bfloat16 [65536, 512], P(('dom', 'gp')), may hold values from -6 to 6
Outputs:
- grad_atoms: bfloat16 [65536, 512], P(('dom', 'gp'))
- grad_wa: float32 [512, 512], replicated
- grad_wd: float32 [512, 64], replicated
- grad_wt: float32 [64, 512], replicated
- grad_wb: float32 [512, 512], replicated
Inputs may be any that keep to these rules, and one draw needn't show every extreme that they name: `edge_src`: row of the device's slab table: ghost rows of the lower slab, then the slab's 1024 atoms, then ghost rows of the upper slab. `trip_in`: slot of the device's own edges. `trip_out`: slot of the device's own edges. `edge_count`: some device has all 2048 slots valid; counts differ widely between devices. `trip_count`: some device has all 2048 slots valid; counts differ widely between devices.
All inputs are finite; a program needn't handle non-finite values.
Results may differ from a plain program's by a relative error of at most 0.011.
Values may be sent and summed in bfloat16 or wider, within the bound.
A program may use at most 128 MiB of HBM per device.

v0:
```python
import math

import jax
import jax.numpy as jnp
from jax import lax
from jax.sharding import PartitionSpec as P

GH = 128


def from_behind(block, axis, distance):
    devices = range(lax.axis_size(axis))
    route = [((i - distance) % len(devices), i) for i in devices]
    return lax.ppermute(block, axis, route)


def edge_pass(
    table_rows, edge_feats, sources, trip_src, trip_dst, basis, edge_valid, trip_valid, w_down, w_up
):
    slots = sources.shape[0]
    edge_mask = (jnp.arange(slots) < edge_valid).astype(jnp.float32)[:, None]
    trip_mask = (jnp.arange(trip_src.shape[0]) < trip_valid).astype(jnp.float32)[:, None]
    incoming = edge_mask * (
        table_rows[sources].astype(jnp.float32) + edge_feats.astype(jnp.float32)
    )
    down = jnp.dot(incoming, w_down.astype(jnp.float32), precision=lax.Precision.HIGHEST)
    trip_weight = basis.astype(jnp.float32) * trip_mask
    summed = jax.ops.segment_sum(trip_weight * down[trip_src], trip_dst, num_segments=slots).astype(
        jnp.bfloat16
    )
    preact = incoming + jnp.dot(summed, w_up, preferred_element_type=jnp.float32)
    outgoing = edge_mask * jax.nn.silu(preact)
    return (edge_mask, trip_weight, incoming, summed, preact, outgoing)


def edge_back(
    edge_mask,
    trip_weight,
    incoming,
    summed,
    preact,
    atom_grad,
    targets,
    sources,
    trip_src,
    trip_dst,
    w_down,
    w_up,
    table_len,
):
    slots = sources.shape[0]
    sigma = jax.nn.sigmoid(preact)
    dpre = edge_mask * atom_grad[targets] * sigma * (1.0 + preact * (1.0 - sigma))
    dsum = jnp.dot(dpre, w_up.astype(jnp.float32).T, precision=lax.Precision.HIGHEST)
    grad_up = jnp.dot(summed.astype(jnp.float32).T, dpre, precision=lax.Precision.HIGHEST)
    ddown = jax.ops.segment_sum(trip_weight * dsum[trip_dst], trip_src, num_segments=slots)
    grad_down = jnp.dot(incoming.T, ddown, precision=lax.Precision.HIGHEST)
    dincoming = edge_mask * (
        dpre + jnp.dot(ddown, w_down.astype(jnp.float32).T, precision=lax.Precision.HIGHEST)
    )
    dtable = jax.ops.segment_sum(dincoming, sources, num_segments=table_len)
    return (dtable, grad_down, grad_up)


def extend(rows):
    owned = rows.shape[0]
    width = rows.shape[1]
    groups = lax.axis_size("gp")
    whole = lax.all_gather(rows, "gp", axis=0, tiled=True)
    shards = whole.reshape(groups, owned, width)
    tails = shards[:, owned - GH :].reshape(groups * GH, width)
    heads = shards[:, :GH].reshape(groups * GH, width)
    lower_set = from_behind(tails, "dom", 1)
    upper_set = from_behind(heads, "dom", -1)
    return jnp.concatenate([lower_set, whole, upper_set], 0)


def retract(partial_value):
    groups = lax.axis_size("gp")
    width = partial_value.shape[1]
    rim = groups * GH
    slab_rows = partial_value.shape[0] - 2 * rim
    owned = slab_rows // groups
    lower_part = partial_value[:rim]
    middle = partial_value[rim : rim + slab_rows]
    upper_part = partial_value[rim + slab_rows :]
    to_tails = from_behind(lower_part.astype(jnp.bfloat16), "dom", -1).astype(lower_part.dtype)
    to_heads = from_behind(upper_part.astype(jnp.bfloat16), "dom", 1).astype(upper_part.dtype)
    shards = middle.reshape(groups, owned, width)
    shards = shards.at[:, owned - GH :].add(to_tails.reshape(groups, GH, width))
    shards = shards.at[:, :GH].add(to_heads.reshape(groups, GH, width))
    return lax.psum_scatter(shards.reshape(slab_rows, width), "gp", scatter_dimension=0, tiled=True)


def per_device(
    atoms,
    messages,
    edge_src,
    edge_dst,
    trip_in,
    trip_out,
    trip_basis,
    edge_count,
    trip_count,
    w_a,
    w_down,
    w_t,
    w_b,
    cotangent,
):
    groups = lax.axis_size("gp")
    slabs = lax.axis_size("dom")
    owned = atoms.shape[0]
    slab_rows = owned * groups
    table_rows = extend(
        jnp.dot(atoms, w_a, preferred_element_type=jnp.float32).astype(jnp.bfloat16)
    )
    table_len = table_rows.shape[0]
    edge_mask, trip_weight, incoming, summed, preact, outgoing = edge_pass(
        table_rows,
        messages,
        edge_src,
        trip_in,
        trip_out,
        trip_basis,
        edge_count[0],
        trip_count[0],
        w_down,
        w_t,
    )
    atom_part = jax.ops.segment_sum(outgoing, edge_dst, num_segments=slab_rows)
    atom_sum = lax.psum_scatter(
        atom_part.astype(jnp.bfloat16), "gp", scatter_dimension=0, tiled=True
    ).astype(jnp.float32)
    own_grad = jnp.dot(cotangent, w_b.T, preferred_element_type=jnp.float32)
    slab_grad = lax.all_gather(own_grad, "gp", axis=0, tiled=True)
    dtable, grad_down, grad_up = edge_back(
        edge_mask,
        trip_weight,
        incoming,
        summed,
        preact,
        slab_grad,
        edge_dst,
        edge_src,
        trip_in,
        trip_out,
        w_down,
        w_t,
        table_len,
    )
    dproj = retract(dtable)
    grad_own = jnp.dot(dproj, w_a.astype(jnp.float32).T, precision=lax.Precision.HIGHEST)
    grad_wa = jnp.dot(atoms.astype(jnp.float32).T, dproj, precision=lax.Precision.HIGHEST)
    grad_wb = jnp.dot(atom_sum.T, cotangent.astype(jnp.float32), precision=lax.Precision.HIGHEST)
    grad_wa, grad_down, grad_up, grad_wb = lax.psum(
        (grad_wa, grad_down, grad_up, grad_wb), ("dom", "gp")
    )
    factor = 1.0 / math.sqrt(owned * groups * slabs)
    return (
        grad_own.astype(jnp.bfloat16),
        grad_wa * factor,
        grad_down * factor,
        grad_up * factor,
        grad_wb * factor,
    )


def solution(mesh):
    in_specs = (
        P(("dom", "gp"), None),
        P(("dom", "gp"), None),
        P(("dom", "gp")),
        P(("dom", "gp")),
        P(("dom", "gp")),
        P(("dom", "gp")),
        P(("dom", "gp"), None),
        P(("dom", "gp")),
        P(("dom", "gp")),
        P(),
        P(),
        P(),
        P(),
        P(("dom", "gp"), None),
    )
    out_specs = (P(("dom", "gp"), None), P(), P(), P(), P())
    return jax.shard_map(
        per_device, mesh=mesh, in_specs=in_specs, out_specs=out_specs, check_vma=False
    )
```

profile of v0, /device:TPU:1, one launch (start us, length us, event | category | flops | bytes accessed | tf_op | source)
XLA Modules:
  0.0 530.4 jit_solution(5831245121020291096)
XLA Ops:
  10.2 2.3 fusion.38
  15.8 22.2 %all-gather.5.cloned.1.call-done = bf16[1024,512]{1,0:T(8,128)(2,1)} async-done(((bf16[256,512]{1,0:T(8,128)(2,1)}), bf16[1024,512]{1,0:T(8,128)(2,1)}) %all-gather.5.cloned.1.call-update) | async-done | bytes 1048592 | tf_op jit(solution)/shard_map/all_gather | solution.py:69
  39.3 7.6 %collective-permute-start.1 = (bf16[512,512]{1,0:T(8,128)(2,1)S(1)}, bf16[512,512]{1,0:T(8,128)(2,1)S(1)}, u32[]{:S(2)}, u32[]{:S(2)}) collective-permute-start(bf16[512,512]{1,0:T(8,128)(2,1)S(1)} %bitcast.39), channel_id=1, source_target_pairs={{4,0},{8,4},{12,8},{16,12},{20,16},{24,20},{28,24},{32,28},{36,32}... | collective-permute-start | bytes 1572872 | tf_op jit(solution)/shard_map/ppermute | solution.py:14
  46.9 17.5 %collective-permute-done.1 = bf16[512,512]{1,0:T(8,128)(2,1)S(1)} collective-permute-done((bf16[512,512]{1,0:T(8,128)(2,1)S(1)}, bf16[512,512]{1,0:T(8,128)(2,1)S(1)}, u32[]{:S(2)}, u32[]{:S(2)}) %collective-permute-start.1) | collective-permute-done | bytes 524320 | tf_op jit(solution)/shard_map/ppermute | solution.py:14
  64.4 16.5 %collective-permute-done = bf16[512,512]{1,0:T(8,128)(2,1)S(1)} collective-permute-done((bf16[512,512]{1,0:T(8,128)(2,1)S(1)}, bf16[512,512]{1,0:T(8,128)(2,1)S(1)}, u32[]{:S(2)}, u32[]{:S(2)}) %collective-permute-start) | collective-permute-done | bytes 524320 | tf_op jit(solution)/shard_map/ppermute | solution.py:14
  82.3 9.2 %gather_fusion.1 = bf16[2048,512]{1,0:T(8,128)(2,1)} fusion(bf16[2048,512]{1,0:T(8,128)(2,1)S(1)} %pad_maximum_fusion, s32[2048]{0:T(1024)S(1)} %fusion.29), kind=kCustom, calls=%fused_computation.1 | custom fusion | bytes 4202496 | tf_op jit(solution)/shard_map/gather | solution.py:24
  91.4 4.7 fusion.7
  96.2 18.9 %scatter_custom_fusion = f32[2048,64]{1,0:T(8,128)} fusion(s32[2048]{0:T(1024)S(1)} %copy-done.15, bf16[2048,64]{1,0:T(8,128)(2,1)S(1)} %copy.19, f32[2048]{0:T(1024)S(1)} %fusion.33, f32[]{:T(128)} %constant.65.clone.1, f32[2048,64]{1,0:T(8,128)S(1)} %fusion.7, s32[2048]{0:T(1024)S(1)} %fusion.30), kind=kCustom, calls=%fused_computation.37 | custom fusion | flops 524288 | bytes 2113540 | tf_op jit(solution)/shard_map/scatter-add | solution.py:28
  115.1 11.3 %gather_fusion = f32[2048,512]{1,0:T(8,128)} fusion(f32[1024,512]{1,0:T(8,128)} %all-gather.3.cloned.1.call-done, s32[2048]{0:T(1024)S(1)} %fusion.28), kind=kCustom, calls=%fused_computation | custom fusion | bytes 8396800 | tf_op jit(solution)/shard_map/gather | solution.py:53
  126.3 6.7 %add_multiply_fusion = (f32[2048,512]{1,0:T(8,128)}, f32[2048,512]{1,0:T(8,128)}) fusion(f32[2048,512]{1,0:T(8,128)} %gather_fusion, f32[2048]{0:T(1024)S(1)} %fusion.32, bf16[64,512]{1,0:T(8,128)(2,1)S(1)} %copy-done.13, f32[2048,64]{1,0:T(8,128)} %scatter_custom_fusion, bf16[2048,512]{1,0:T(8,128)(2,1)} %param.19, bf16[2048,512]{1,0:T(8,128)(2,1)S(1)} %copy-done.2), kind=kOutput, calls=%fused_computation.14 | convolution fusion | flops 149028864 | bytes 17375232 | tf_op jit(solution)/shard_map/dot_general | solution.py:31
  133.0 15.4 %scatter_custom_fusion.3 = f32[1024,512]{1,0:T(8,128)S(1)} fusion(s32[2048]{0:T(1024)S(1)} %copy-done.14, f32[2048,512]{1,0:T(8,128)} %get-tuple-element.43, f32[]{:T(128)} %constant.68.clone.1, f32[2048]{0:T(1024)S(1)} %fusion.32, f32[]{:T(128)} %constant.65.clone.1), kind=kCustom, calls=%fused_computation.8 | custom fusion | flops 6291456 | bytes 6299656 | tf_op jit(solution)/shard_map/scatter-add | solution.py:131
  149.6 4.1 fusion.39
  153.8 18.4 %scatter_custom_fusion.1 = f32[2048,64]{1,0:T(8,128)S(1)} fusion(s32[2048]{0:T(1024)S(1)} %copy-done.16, bf16[2048,64]{1,0:T(8,128)(2,1)S(1)} %copy.19, f32[2048]{0:T(1024)S(1)} %fusion.33, f32[]{:T(128)} %constant.65.clone.1, f32[2048,64]{1,0:T(8,128)S(1)} %fusion.39, s32[2048]{0:T(1024)S(1)} %fusion.31), kind=kCustom, calls=%fused_computation.35 | custom fusion | flops 524288 | bytes 2113540 | tf_op jit(solution)/shard_map/scatter-add | solution.py:56
  172.2 3.8 fusion.40
  175.9 16.8 %scatter_custom_fusion.2 = f32[2048,512]{1,0:T(8,128)} fusion(s32[2048]{0:T(1024)} %param.20, f32[2048,512]{1,0:T(8,128)} %get-tuple-element.42, f32[2048,512]{1,0:T(8,128)} %fusion.40, f32[2048]{0:T(1024)S(1)} %fusion.32, f32[]{:T(128)} %constant.65.clone.1), kind=kCustom, calls=%fused_computation.11 | custom fusion | flops 3145728 | bytes 12591616 | tf_op jit(solution)/shard_map/scatter-add | solution.py:61
  192.8 2.5 convert.10
  196.9 8.9 %collective-permute-done.2 = bf16[512,512]{1,0:T(8,128)(2,1)S(1)} collective-permute-done((bf16[512,512]{1,0:T(8,128)(2,1)S(1)}, bf16[512,512]{1,0:T(8,128)(2,1)S(1)}, u32[]{:S(2)}, u32[]{:S(2)}) %collective-permute-start.2) | collective-permute-done | bytes 524320 | tf_op jit(solution)/shard_map/ppermute | solution.py:14
  206.1 18.1 %collective-permute-done.3 = bf16[512,512]{1,0:T(8,128)(2,1)S(1)} collective-permute-done((bf16[512,512]{1,0:T(8,128)(2,1)S(1)}, bf16[512,512]{1,0:T(8,128)(2,1)S(1)}, u32[]{:S(2)}, u32[]{:S(2)}) %collective-permute-start.3) | collective-permute-done | bytes 524320 | tf_op jit(solution)/shard_map/ppermute | solution.py:14
  226.2 5.0 fusion.25
  231.2 3.9 fusion.6
  235.1 2.3 fusion.41
  237.3 13.1 %reduce-scatter.3.cloned.1.call-done = f32[256,512]{1,0:T(8,128)} async-done(((f32[1024,512]{1,0:T(8,128)}), f32[256,512]{1,0:T(8,128)}) %reduce-scatter.3.cloned.1.call-update) | async-done | bytes 524304 | tf_op jit(solution)/shard_map/reduce_scatter | solution.py:92
  250.4 2.7 convolution_bitcast_fusion
  254.5 263.5 %all-reduce.3.cloned.1.call-done = (f32[512,512]{0,1:T(8,128)}, f32[512,64]{0,1:T(8,128)}, f32[64,512]{1,0:T(8,128)}, f32[512,512]{0,1:T(8,128)}) async-done(((f32[512,512]{0,1:T(8,128)}, f32[512,64]{0,1:T(8,128)}, f32[64,512]{1,0:T(8,128)}, f32[512,512]{0,1:T(8,128)}), (f32[512,512]{0,1:T(8,128)}, f32[512,64]{0,1:T(8,128)}, f32[64,512]{1,0:T(8,128)}, f32[512,512]{0,1:T(8,128)})) %all-reduce.3.cloned.1.call-update) | async-done | bytes 2359312 | tf_op jit(solution)/shard_map/psum | solution.py:156
  (71 shorter events, 19.9 us)
Async XLA Ops:
  7.2 39.7 %copy-start.14 = (s32[2048]{0:T(1024)S(1)}, s32[2048]{0:T(1024)}, u32[]{:S(2)}) copy-start(s32[2048]{0:T(1024)} %param.21) | copy-start | bytes 24580
  7.2 39.7 %copy-start.16 = (s32[2048]{0:T(1024)S(1)}, s32[2048]{0:T(1024)}, u32[]{:S(2)}) copy-start(s32[2048]{0:T(1024)} %param.22) | copy-start | bytes 24580
  7.2 30.8 %all-gather.5.cloned.1.call-start = ((), (), s32[]{:S(2)}) async-start(), calls=%async_computation.3 | async-start | bytes 1310720 | tf_op jit(solution)/shard_map/all_gather | solution.py:69
  10.2 104.9 %all-gather.3.cloned.1.call-start = ((), (), s32[]{:S(2)}) async-start(), calls=%async_computation.2 | async-start | bytes 2621440 | tf_op jit(solution)/shard_map/all_gather | solution.py:136
  12.5 222.5 %reduce-scatter.5.cloned.1.call-start = ((), (), s32[]{:S(2)}) async-start(), calls=%async_computation.5 | async-start | bytes 1310720 | tf_op jit(solution)/shard_map/reduce_scatter | solution.py:132
  39.3 25.1 %collective-permute-start.1 = (bf16[512,512]{1,0:T(8,128)(2,1)S(1)}, bf16[512,512]{1,0:T(8,128)(2,1)S(1)}, u32[]{:S(2)}, u32[]{:S(2)}) collective-permute-start(bf16[512,512]{1,0:T(8,128)(2,1)S(1)} %bitcast.39), channel_id=1, source_target_pairs={{4,0},{8,4},{12,8},{16,12},{20,16},{24,20},{28,24},{32,28},{36,32}... | collective-permute-start | bytes 1572872 | tf_op jit(solution)/shard_map/ppermute | solution.py:14
  46.9 34.0 %collective-permute-start = (bf16[512,512]{1,0:T(8,128)(2,1)S(1)}, bf16[512,512]{1,0:T(8,128)(2,1)S(1)}, u32[]{:S(2)}, u32[]{:S(2)}) collective-permute-start(bf16[512,512]{1,0:T(8,128)(2,1)S(1)} %bitcast.38), channel_id=1, source_target_pairs={{252,0},{0,4},{4,8},{8,12},{12,16},{16,20},{20,24},{24,28},{28,32}... | collective-permute-start | bytes 1572872 | tf_op jit(solution)/shard_map/ppermute | solution.py:14
  82.2 9.2 %copy-start.10 = (bf16[512,64]{0,1:T(8,128)(2,1)S(1)}, bf16[512,64]{0,1:T(8,128)(2,1)}, u32[]{:S(2)}) copy-start(bf16[512,64]{0,1:T(8,128)(2,1)} %param.28) | copy-start | bytes 196612
  91.4 4.7 copy-start.15
  115.1 11.3 %copy-start.2 = (bf16[2048,512]{1,0:T(8,128)(2,1)S(1)}, bf16[2048,512]{1,0:T(8,128)(2,1)}, u32[]{:S(2)}) copy-start(bf16[2048,512]{1,0:T(8,128)(2,1)} %gather_fusion.1) | copy-start | bytes 6291460
  115.1 11.3 %copy-start.13 = (bf16[64,512]{1,0:T(8,128)(2,1)S(1)}, bf16[64,512]{1,0:T(8,128)(2,1)}, u32[]{:S(2)}) copy-start(bf16[64,512]{1,0:T(8,128)(2,1)} %param.29) | copy-start | bytes 196612
  149.6 100.9 %reduce-scatter.3.cloned.1.call-start = ((), (), s32[]{:S(2)}) async-start(), calls=%async_computation.4 | async-start | bytes 2621440 | tf_op jit(solution)/shard_map/reduce_scatter | solution.py:92
  172.2 20.6 %copy-start.4 = (f32[2048,64]{1,0:T(8,128)}, f32[2048,64]{1,0:T(8,128)S(1)}, u32[]{:S(2)}) copy-start(f32[2048,64]{1,0:T(8,128)S(1)} %scatter_custom_fusion.1) | copy-start | bytes 1572868
  195.2 10.6 %slice-start = ((f32[2048,512]{1,0:T(8,128)}), f32[1024,512]{1,0:T(8,128)S(1)}, s32[]{:S(2)}) async-start(f32[2048,512]{1,0:T(8,128)} %scatter_custom_fusion.2), calls=%async_computation.7 | async-start | bytes 4194304 | tf_op jit(solution)/shard_map/slice | solution.py:85
  195.3 10.5 %collective-permute-start.2 = (bf16[512,512]{1,0:T(8,128)(2,1)S(1)}, bf16[512,512]{1,0:T(8,128)(2,1)S(1)}, u32[]{:S(2)}, u32[]{:S(2)}) collective-permute-start(bf16[512,512]{1,0:T(8,128)(2,1)S(1)} %get-tuple-element.39), channel_id=1, source_target_pairs={{4,0},{8,4},{12,8},{16,12},{20,16},{24,20},{28,24},{32,28},{36,32}... | collective-permute-start | bytes 1572872 | tf_op jit(solution)/shard_map/ppermute | solution.py:14
  195.4 28.8 %collective-permute-start.3 = (bf16[512,512]{1,0:T(8,128)(2,1)S(1)}, bf16[512,512]{1,0:T(8,128)(2,1)S(1)}, u32[]{:S(2)}, u32[]{:S(2)}) collective-permute-start(bf16[512,512]{1,0:T(8,128)(2,1)S(1)} %get-tuple-element.38), channel_id=1, source_target_pairs={{252,0},{0,4},{4,8},{8,12},{12,16},{16,20},{20,24},{24,28},{28,32}... | collective-permute-start | bytes 1572872 | tf_op jit(solution)/shard_map/ppermute | solution.py:14
  225.8 5.3 %copy-start.3 = (bf16[2048,512]{1,0:T(8,128)(2,1)S(1)}, bf16[2048,512]{1,0:T(8,128)(2,1)}, u32[]{:S(2)}) copy-start(bf16[2048,512]{1,0:T(8,128)(2,1)} %gather_fusion.1) | copy-start | bytes 6291460
  225.8 292.2 %all-reduce.3.cloned.1.call-start = ((), (), s32[]{:S(2)}) async-start(), calls=%async_computation.6 | async-start | bytes 4718592 | tf_op jit(solution)/shard_map/psum | solution.py:156
  226.1 5.0 copy-start.5
  226.2 5.0 copy-start.6
  226.2 8.9 %copy-start.8 = (bf16[256,512]{1,0:T(8,128)(2,1)S(1)}, bf16[256,512]{1,0:T(8,128)(2,1)}, u32[]{:S(2)}) copy-start(bf16[256,512]{1,0:T(8,128)(2,1)} %param.31) | copy-start | bytes 786436
  231.2 19.2 %copy-start.9 = (bf16[256,512]{1,0:T(8,128)(2,1)S(1)}, bf16[256,512]{1,0:T(8,128)(2,1)}, u32[]{:S(2)}) copy-start(bf16[256,512]{1,0:T(8,128)(2,1)} %param.18) | copy-start | bytes 786436
  518.0 3.2 copy-start.12
  518.0 3.8 copy-start.11
  (3 other events, 5.1 us)
Sparse Core Ops, SparseCore 0:
  10.4 27.5 all-gather.4
  40.4 47.2 all-gather.2
  149.7 16.8 reduce-scatter.4
  225.9 24.4 reduce-scatter.2
  256.7 261.2 all-reduce.2
where the time goes:
time: 531 us; the launch traced here: 530 us
  waiting for transfers between devices  360 us (68%)
  other arithmetic  78.9 us (15%)
  matrix products  38.7 us (7%)
  local copies, waits for them, and re-layouts  28 us (5%)
  between operations  15.3 us (3%)
  starting transfers between devices  9.58 us (2%)
    psum x1, waiting for transfers between devices, per_device(): lax.psum((grad_wa, grad_down, grad_up, grad_wb), ('dom', 'gp'))  264 us
    ppermute x4, waiting for transfers between devices, from_behind(): return lax.ppermute(block, axis, route)  61 us
    all_gather x1, waiting for transfers between devices, extend(): whole = lax.all_gather(rows, 'gp', axis=0, tiled=True)  22.2 us
    scatter-add x1, other arithmetic, edge_pass(): jax.ops.segment_sum(trip_weight * down[trip_src], trip_dst, num_segments=...  18.9 us
    scatter-add x1, other arithmetic, edge_back(): jax.ops.segment_sum(trip_weight * dsum[trip_dst], trip_src, num_segments=...  18.4 us
    scatter-add x1, other arithmetic, edge_back(): dtable = jax.ops.segment_sum(dincoming, sources, num_segments=table_len)  16.8 us
    scatter-add x1, other arithmetic, per_device(): atom_part = jax.ops.segment_sum(outgoing, edge_dst, num_segments=slab_rows)  15.4 us
    reduce_scatter x1, waiting for transfers between devices, retract(): lax.psum_scatter(shards.reshape(slab_rows, width), 'gp', scatter_dimensio...  13.1 us
  transfers between devices with their start and end apart: 9, of which 7 were waited for; matrix products, arithmetic and copies ran while one was open for 19% of the time, Pallas kernels for 0%

commit v1 on v0

v1 whole, which is shorter than its diff:
```python
import functools
import math

import jax
import jax.numpy as jnp
from jax import lax
from jax.experimental import pallas as pl
from jax.experimental.pallas import tpu as pltpu
from jax.sharding import PartitionSpec as P

BF = jnp.bfloat16
F32 = jnp.float32
MESH = pl.DeviceIdType.MESH
GH = 128
OWN = 256
ROWS = 512
SLOTS = 2048
WIDTH = 512
DT = 64
LO = 256
BLK = 512
PIECE = 144


def dims_of(slabs):
    return {64: (4, 4, 4), 4: (1, 1, 4), 2: (1, 1, 2)}[slabs]


def nn(a, b):
    return lax.dot_general(a, b, (((1,), (0,)), ((), ())), preferred_element_type=F32)


def nt(a, b):
    return lax.dot_general(a, b, (((1,), (1,)), ((), ())), preferred_element_type=F32)


def tn(a, b):
    return lax.dot_general(a, b, (((0,), (0,)), ((), ())), preferred_element_type=F32)


def lanes(shape):
    return lax.broadcasted_iota(jnp.int32, shape, len(shape) - 1)


def pick_columns(index, first, width):
    lane = lanes(index.shape)
    local = index - first
    return jnp.concatenate(
        [jnp.where(local == lane + 128 * j, 1.0, 0.0).astype(BF) for j in range(width // 128)], axis=1
    )


def pick_rows(index, first, height):
    shape = (height, index.shape[1])
    row = lax.broadcasted_iota(jnp.int32, shape, 0)
    return jnp.where(row == jnp.broadcast_to(index - first, shape), 1.0, 0.0).astype(BF)


def table_row(src):
    lower = ((src >> 7) << 9) + (src & 127)
    mid = src - 512
    middle = ((mid >> 8) << 9) + GH + (mid & 255)
    up = src - 1536
    upper = ((up >> 7) << 9) + GH + OWN + (up & 127)
    return jnp.where(src < 512, lower, jnp.where(src < 1536, middle, upper))


def kernel(
    dims,
    ecnt_ref, tcnt_ref, src_ref, dst_ref, tin_ref, tout_ref,
    atoms_ref, cot_ref, msg_hbm, basis_ref, wa_ref, wdown_ref, wt_ref, wb_ref,
    full_out, grad_out,
    table, cots, msg, picked, inc, dpre, dinc, dtable, rd, ed, re, own_sum, rims_in, rims_out,
    src_col, dst_col, tin_col, tout_col, rows, basis2, wdown2, wt2,
    down, dn, acc_s, sm,
    acc_wa, acc_wb, acc_wt, acc_wd, pieces, rc, half, rx, zbuf, rz_main, rz_small, full,
    send, recv, local_sem,
):
    Y, ZH, X = dims
    XY = X * Y
    Z = 2 * ZH
    nb = 16 // XY
    tile = 128 // Z
    dom = lax.axis_index("dom")
    gp = lax.axis_index("gp")
    slabs = Y * ZH * X
    x = lax.rem(dom, X)
    zh = lax.rem(lax.div(dom, X), ZH)
    y = lax.div(dom, X * ZH)
    core = lax.rem(gp, 2)
    zl = lax.div(gp, 2)
    z = zh * 2 + zl

    sib = {"dom": dom, "gp": zl * 2 + (1 - core)}
    zpart = {"dom": dom, "gp": (1 - zl) * 2 + core}
    kz = (1 - zl) * 2 + core
    above = {"dom": lax.rem(dom + 1, slabs), "gp": gp}
    below = {"dom": lax.rem(dom + slabs - 1, slabs), "gp": gp}
    xy_peers = []
    for j in range(1, XY):
        px = lax.rem(x + j // Y, X)
        py = lax.rem(y + j % Y, Y)
        xy_peers.append((px * Y + py, {"dom": (py * ZH + zh) * X + px, "gp": gp}))
    z_peers = []
    for j in range(1, Z):
        pz = lax.rem(z + j, Z)
        z_peers.append((pz, {"dom": (y * ZH + lax.div(pz, 2)) * X + x, "gp": lax.rem(pz, 2) * 2 + core}))

    barrier = pltpu.get_barrier_semaphore()
    others = [sib, above, below] + [d for _, d in xy_peers] + [d for _, d in z_peers]
    for d in others:
        pl.semaphore_signal(barrier, inc=1, device_id=d, device_id_type=MESH)

    count = [0]
    started = []

    def remote(src, dst, device):
        i = count[0]
        count[0] += 1
        c = pltpu.make_async_remote_copy(
            src_ref=src, dst_ref=dst, send_sem=send.at[i], recv_sem=recv.at[i],
            device_id=device, device_id_type=MESH,
        )
        c.start()
        started.append(c)
        return c

    msg_copy = pltpu.make_async_copy(msg_hbm, msg, local_sem.at[0])
    msg_copy.start()
    pl.semaphore_wait(barrier, len(others))

    mid = pl.ds(GH, OWN)
    low = pl.ds(0, GH)
    high = pl.ds(GH + OWN, GH)
    to_z = remote(atoms_ref, table.at[gp, mid], zpart)
    to_above = remote(atoms_ref.at[pl.ds(OWN - GH, GH)], table.at[gp, low], above)
    to_below = remote(atoms_ref.at[pl.ds(0, GH)], table.at[gp, high], below)
    to_sib = remote(atoms_ref, table.at[gp, mid], sib)
    table[gp, mid] = atoms_ref[...]
    cots[gp] = cot_ref[...]

    edges = ecnt_ref[0]
    trips = tcnt_ref[0]
    for n, (ref, col) in enumerate(
        ((src_ref, src_col), (dst_ref, dst_col), (tin_ref, tin_col), (tout_ref, tout_col))
    ):
        flat = ref[...]
        if n == 0:
            flat = table_row(flat)
        for j in range(SLOTS // 128):
            line = flat[j : j + 1]
            rows[n : n + 1, 128 * j : 128 * (j + 1)] = line
            col[128 * j : 128 * (j + 1)] = jnp.transpose(jnp.broadcast_to(line, (128, 128)))
    twice = jnp.where(
        lax.broadcasted_iota(jnp.int32, (DT, 128), 0) == (lanes((DT, 128)) & (DT - 1)), 1.0, 0.0
    ).astype(BF)
    valid = lax.broadcasted_iota(jnp.int32, (SLOTS, 128), 0) < trips
    basis2[...] = jnp.where(valid, nn(basis_ref[...], twice), 0.0)
    wdown2[...] = nn(wdown_ref[...], twice).astype(BF)
    wt2[...] = jnp.concatenate([wt_ref[...], wt_ref[...]], axis=0)

    to_above.wait_recv()
    z_low = remote(table.at[gp, low], table.at[gp, low], zpart)
    s_low = remote(table.at[gp, low], table.at[gp, low], sib)
    to_below.wait_recv()
    z_high = remote(table.at[gp, high], table.at[gp, high], zpart)
    s_high = remote(table.at[gp, high], table.at[gp, high], sib)
    z_cot = remote(cot_ref, cots.at[gp], zpart)
    s_cot = remote(cot_ref, cots.at[gp], sib)
    to_z.wait_recv()
    f_mid = remote(table.at[kz, mid], table.at[kz, mid], sib)
    z_low.wait_recv()
    f_low = remote(table.at[kz, low], table.at[kz, low], sib)
    z_high.wait_recv()
    f_high = remote(table.at[kz, high], table.at[kz, high], sib)
    msg_copy.wait()
    for c in (to_sib, s_low, s_high, f_mid, f_low, f_high):
        c.wait_recv()

    def row_mask(start, n, width):
        return lax.broadcasted_iota(jnp.int32, (n, width), 0) + start < edges

    def edge_in(b, carry):
        at = pl.ds(pl.multiple_of(b * BLK, BLK), BLK)
        index = src_col[at]
        got = nn(pick_columns(index, 0, ROWS), table[0])
        for k in range(1, 4):
            got = got + nn(pick_columns(index, k * ROWS, ROWS), table[k])
        got = got.astype(BF)
        picked[at] = got
        proj = nn(got, wa_ref[...]).astype(BF).astype(F32)
        value = jnp.where(row_mask(b * BLK, BLK, WIDTH), proj + msg[at].astype(F32), 0.0)
        inc[at] = value
        down[at] = nn(value.astype(BF), wdown2[...]).astype(BF)
        return carry

    lax.fori_loop(0, SLOTS // BLK, edge_in, 0)
    z_cot.wait_recv()
    f_cot = remote(cots.at[kz], cots.at[kz], sib)

    def pack(source):
        first = lanes((LO, 128)) < DT
        for j in range(4):
            a = source[2 * j * LO : (2 * j + 1) * LO].astype(F32)
            b = source[(2 * j + 1) * LO : (2 * j + 2) * LO].astype(F32)
            dn[:, 128 * j : 128 * (j + 1)] = jnp.where(first, a, b).astype(BF)

    def unpack():
        first = lanes((LO, 128)) < DT
        for j in range(4):
            v = acc_s[:, 128 * j : 128 * (j + 1)]
            sm[2 * j * LO : (2 * j + 1) * LO] = jnp.where(first, v, 0.0).astype(BF)
            sm[(2 * j + 1) * LO : (2 * j + 2) * LO] = jnp.where(first, 0.0, v).astype(BF)

    def triplets(from_col, to_col, to_row):
        half_lane = jnp.where(lanes((BLK, 128)) < DT, 0, 1)
        acc_s[...] = jnp.zeros_like(acc_s)

        def body(b, carry):
            at = pl.ds(pl.multiple_of(b * BLK, BLK), BLK)
            frm = from_col[at]
            to = to_col[at]
            got = nn(pick_columns(frm & (LO - 1), 0, LO), dn[...])
            frm_hi = frm >> 8
            to_hi = to >> 8
            value = jnp.where(frm_hi == half_lane, got[:, 0:128], 0.0)
            for j in range(1, 4):
                value = value + jnp.where(
                    frm_hi == half_lane + 2 * j, got[:, 128 * j : 128 * (j + 1)], 0.0
                )
            value = value + pltpu.roll(value, DT, 1)
            value = value * basis2[at]
            spread = jnp.concatenate(
                [jnp.where(to_hi == half_lane + 2 * j, value, 0.0).astype(BF) for j in range(4)], axis=1
            )
            line = rows[to_row : to_row + 1, pl.ds(pl.multiple_of(b * BLK, BLK), BLK)]
            acc_s[...] += nn(pick_rows(line & (LO - 1), 0, LO), spread)
            return carry

        lax.fori_loop(0, SLOTS // BLK, body, 0)

    pack(down)
    triplets(tin_col, tout_col, 3)
    unpack()
    s_cot.wait_recv()
    f_cot.wait_recv()

    acc_wb[...] = jnp.zeros_like(acc_wb)
    acc_wt[...] = jnp.zeros_like(acc_wt)

    def edge_mid(b, carry):
        at = pl.ds(pl.multiple_of(b * BLK, BLK), BLK)
        mask = row_mask(b * BLK, BLK, WIDTH)
        index = dst_col[at]
        cot = nn(pick_columns(index, 0, OWN), cots[0])
        for k in range(1, 4):
            cot = cot + nn(pick_columns(index, k * OWN, OWN), cots[k])
        cot = cot.astype(BF)
        atom_grad = nt(cot, wb_ref[...])
        summed = sm[at]
        pre = inc[at] + nn(summed, wt2[...])
        sig = jax.nn.sigmoid(pre)
        out = jnp.where(mask, pre * sig, 0.0).astype(BF)
        grad = jnp.where(mask, atom_grad * sig * (1.0 + pre * (1.0 - sig)), 0.0)
        dpre[at] = grad
        grad = grad.astype(BF)
        acc_wb[...] += tn(out, cot)
        acc_wt[...] += tn(summed, grad)
        down[at] = nt(grad, wt2[...]).astype(BF)
        return carry

    lax.fori_loop(0, SLOTS // BLK, edge_mid, 0)

    pack(down)
    triplets(tout_col, tin_col, 2)
    unpack()

    acc_wa[...] = jnp.zeros_like(acc_wa)
    acc_wd[...] = jnp.zeros_like(acc_wd)

    def edge_out(b, carry):
        at = pl.ds(pl.multiple_of(b * BLK, BLK), BLK)
        mask = row_mask(b * BLK, BLK, WIDTH)
        back = sm[at]
        grad = jnp.where(mask, dpre[at] + nt(back, wdown2[...]), 0.0).astype(BF)
        dinc[at] = grad
        acc_wd[...] += tn(back, inc[at].astype(BF))
        acc_wa[...] += tn(picked[at], grad)
        return carry

    lax.fori_loop(0, SLOTS // BLK, edge_out, 0)

    for s in range(32):
        big, small = (acc_wa, acc_wt) if s < 16 else (acc_wb, acc_wd)
        r, c = (s % 16) // 4, s % 4
        cols = slice(128 * c, 128 * (c + 1))
        pieces[s, 0:128] = big[128 * r : 128 * (r + 1), cols].astype(BF)
        pieces[s, 128:144] = (
            small[16 * r : 16 * (r + 1), cols] + small[DT + 16 * r : DT + 16 * (r + 1), cols]
        ).astype(BF)
    w_core = remote(pieces.at[pl.ds((1 - core) * 16, 16)], rc, sib)

    def table_grad(k):
        total = nn(pick_rows(rows[0:1, 0:BLK], k * ROWS, ROWS), dinc[0:BLK])
        for b in range(1, SLOTS // BLK):
            part = slice(BLK * b, BLK * (b + 1))
            total = total + nn(pick_rows(rows[0:1, part], k * ROWS, ROWS), dinc[part])
        dtable[k] = total.astype(BF)

    table_grad(1 - core)
    d_core0 = remote(dtable.at[1 - core], rd.at[0], sib)
    table_grad(3 - core)
    d_core1 = remote(dtable.at[3 - core], rd.at[1], sib)

    w_core.wait_recv()
    mine = pieces[pl.ds(core * 16, 16)].astype(F32) + rc[...].astype(F32)
    half[...] = mine.astype(BF)
    w_xy = [
        remote(half.at[pl.ds(s * nb, nb)], rx.at[j], d) for j, (s, d) in enumerate(xy_peers)
    ]

    def table_grads(i, carry):
        table_grad(2 * i + core)
        return carry

    lax.fori_loop(0, 2, table_grads, 0)
    d_core0.wait_recv()
    d_core1.wait_recv()
    ed[...] = (dtable[kz].astype(F32) + rd[1 - zl].astype(F32)).astype(BF)
    d_z = remote(ed, re, zpart)
    own_sum[...] = dtable[gp].astype(F32) + rd[zl].astype(F32)

    for c in w_xy:
        c.wait_recv()
    own_s = x * Y + y
    total = half[pl.ds(own_s * nb, nb)].astype(F32)
    for j in range(XY - 1):
        total = total + rx[j].astype(F32)
    zbuf[...] = total.astype(BF)
    w_z = []
    for j, (pz, d) in enumerate(z_peers):
        part = pl.ds(pl.multiple_of(pz * tile, tile), tile)
        w_z.append(remote(zbuf.at[:, part], rz_main.at[j + 1], d))
        w_z.append(remote(zbuf.at[:, pl.ds(128, 16)], rz_small.at[j + 1], d))
    own_rows = pl.ds(pl.multiple_of(z * tile, tile), tile)
    rz_small[0] = zbuf[:, 128:144]

    d_z.wait_recv()
    summed_table = own_sum[...] + re[...].astype(F32)
    own_sum[...] = summed_table
    rims_out[0] = summed_table[0:GH].astype(BF)
    rims_out[1] = summed_table[GH + OWN :].astype(BF)
    to_tails = remote(rims_out.at[0], rims_in.at[0], below)
    to_heads = remote(rims_out.at[1], rims_in.at[1], above)

    for c in w_z:
        c.wait_recv()
    total = zbuf[:, own_rows].astype(F32)
    for j in range(1, Z):
        total = total + rz_main[j].astype(F32)
    small = rz_small[lax.rem(Z - z, Z)].astype(F32)
    for j in range(1, Z):
        small = small + rz_small[lax.rem(j + Z - z, Z)].astype(F32)
    own_piece = pl.ds(core * 16 + own_s * nb, nb)
    full[own_piece, own_rows] = total.astype(BF)
    full[own_piece, 128:144] = small.astype(BF)
    g_z = [
        remote(full.at[own_piece, own_rows], full.at[own_piece, own_rows], d) for _, d in z_peers
    ]

    to_tails.wait_recv()
    to_heads.wait_recv()
    dproj = own_sum[GH : GH + OWN] + jnp.concatenate(
        [rims_in[1].astype(F32), rims_in[0].astype(F32)], axis=0
    )
    coarse = dproj.astype(BF)
    fine = (dproj - coarse.astype(F32)).astype(BF)
    grad_out[...] = (nt(coarse, wa_ref[...]) + nt(fine, wa_ref[...])).astype(BF)

    for c in g_z:
        c.wait_recv()
    g_xy = [remote(full.at[own_piece], full.at[own_piece], d) for _, d in xy_peers]
    for c in g_xy:
        c.wait_recv()
    own_core = pl.ds(core * 16, 16)
    g_core = remote(full.at[own_core], full.at[own_core], sib)
    g_core.wait_recv()
    full_out[...] = full[...]
    for c in started:
        c.wait_send()


def finish(factor, full_ref, grad_ref, gatoms_ref, gwa_ref, gwd_ref, gwt_ref, gwb_ref):
    gatoms_ref[...] = grad_ref[...]
    down_rows = []
    for r in range(4):
        for c in range(4):
            s = 4 * r + c
            cols = slice(128 * c, 128 * (c + 1))
            gwa_ref[128 * r : 128 * (r + 1), cols] = full_ref[s, 0:128].astype(F32) * factor
            gwb_ref[128 * r : 128 * (r + 1), cols] = full_ref[s + 16, 0:128].astype(F32) * factor
            gwt_ref[16 * r : 16 * (r + 1), cols] = full_ref[s, 128:144].astype(F32) * factor
    for c in range(4):
        stack = jnp.concatenate(
            [full_ref[16 + 4 * r + c, 128:144].astype(F32) * factor for r in range(4)] * 2, axis=0
        )
        gwd_ref[128 * c : 128 * (c + 1)] = jnp.transpose(stack)[:, 0:DT]


def per_device(
    slabs, groups,
    atoms, messages, edge_src, edge_dst, trip_in, trip_out, trip_basis, edge_count, trip_count,
    w_a, w_down, w_t, w_b, cotangent,
):
    dims = dims_of(slabs)
    Y, ZH, X = dims
    XY, Z = X * Y, 2 * ZH
    nb, tile = 16 // XY, 128 // Z
    transfers = 3 + 1 + 6 + 3 + 1 + 3 + 1 + 2 + 2 * (XY - 1) + 3 * (Z - 1) + 8
    vmem = pl.BlockSpec(memory_space=pltpu.VMEM)
    smem = pl.BlockSpec(memory_space=pltpu.SMEM)
    hbm = pl.BlockSpec(memory_space=pl.ANY)
    index = [a.reshape(16, 128) for a in (edge_src, edge_dst, trip_in, trip_out)]
    V = pltpu.VMEM
    full, grad = pl.pallas_call(
        functools.partial(kernel, dims),
        out_shape=(
            jax.ShapeDtypeStruct((32, PIECE, 128), BF),
            jax.ShapeDtypeStruct((OWN, WIDTH), BF),
        ),
        in_specs=[smem, smem] + [vmem] * 6 + [hbm] + [vmem] * 5,
        out_specs=(vmem, vmem),
        scratch_shapes=[
            V((4, ROWS, WIDTH), BF), V((4, OWN, WIDTH), BF), V((SLOTS, WIDTH), BF),
            V((SLOTS, WIDTH), BF), V((SLOTS, WIDTH), F32), V((SLOTS, WIDTH), F32),
            V((SLOTS, WIDTH), BF), V((4, ROWS, WIDTH), BF), V((2, ROWS, WIDTH), BF),
            V((ROWS, WIDTH), BF), V((ROWS, WIDTH), BF), V((ROWS, WIDTH), F32),
            V((2, GH, WIDTH), BF), V((2, GH, WIDTH), BF),
            V((SLOTS, 128), jnp.int32), V((SLOTS, 128), jnp.int32),
            V((SLOTS, 128), jnp.int32), V((SLOTS, 128), jnp.int32),
            V((8, SLOTS), jnp.int32), V((SLOTS, 128), F32), V((WIDTH, 128), BF), V((128, WIDTH), BF),
            V((SLOTS, 128), BF), V((LO, WIDTH), BF), V((LO, WIDTH), F32), V((SLOTS, 128), BF),
            V((512, WIDTH), F32), V((512, WIDTH), F32), V((128, WIDTH), F32), V((128, WIDTH), F32),
            V((32, PIECE, 128), BF), V((16, PIECE, 128), BF), V((16, PIECE, 128), BF),
            V((XY - 1, nb, PIECE, 128), BF), V((nb, PIECE, 128), BF),
            V((Z, nb, tile, 128), BF), V((Z, nb, 16, 128), BF), V((32, PIECE, 128), BF),
            pltpu.SemaphoreType.DMA((transfers,)), pltpu.SemaphoreType.DMA((transfers,)),
            pltpu.SemaphoreType.DMA((1,)),
        ],
        compiler_params=pltpu.CompilerParams(
            collective_id=0, has_side_effects=True, vmem_limit_bytes=60 * 1024 * 1024
        ),
    )(
        edge_count, trip_count, *index, atoms, cotangent, messages, trip_basis, w_a, w_down, w_t, w_b
    )
    factor = 1.0 / math.sqrt(OWN * groups * slabs)
    return pl.pallas_call(
        functools.partial(finish, factor),
        out_shape=(
            jax.ShapeDtypeStruct((OWN, WIDTH), BF),
            jax.ShapeDtypeStruct((512, WIDTH), F32),
            jax.ShapeDtypeStruct((WIDTH, DT), F32),
            jax.ShapeDtypeStruct((DT, WIDTH), F32),
            jax.ShapeDtypeStruct((512, WIDTH), F32),
        ),
        in_specs=[vmem, vmem],
        out_specs=(vmem,) * 5,
        compiler_params=pltpu.CompilerParams(vmem_limit_bytes=32 * 1024 * 1024),
    )(full, grad)


def solution(mesh):
    both = P(("dom", "gp"))
    rows = P(("dom", "gp"), None)
    in_specs = (rows, rows, both, both, both, both, rows, both, both, P(), P(), P(), P(), rows)
    out_specs = (rows, P(), P(), P(), P())
    return jax.shard_map(
        functools.partial(per_device, mesh.shape["dom"], mesh.shape["gp"]),
        mesh=mesh, in_specs=in_specs, out_specs=out_specs, check_vma=False,
    )
```

time: 531 us -> 111 us (0.21)
  waiting for transfers between devices: 360 us -> 0 us
  Pallas kernels: 0 us -> 102 us
  other arithmetic: 78.9 us -> 0 us
  matrix products: 38.7 us -> 0 us
  local copies, waits for them, and re-layouts: 28 us -> 6.54 us
  between operations: 15.3 us -> 1.94 us
  starting transfers between devices: 9.58 us -> 0 us
    psum x1 -> x0, waiting for transfers between devices: 264 us -> none  [per_device(): lax.psum((grad_wa, grad_down, grad_up, grad_wb), ('dom', 'gp'))]
    pallas_call x0 -> x2, Pallas kernels: none -> 102 us  [the longest x1 100 us: per_device(): pl.pallas_call(functools.partial(kernel, dims), out_shape=(jax.ShapeDtype...]
    scatter-add x6 -> x0, other arithmetic: 70 us -> none  [the longest x1 18.9 us: edge_pass(): jax.ops.segment_sum(trip_weight * down[trip_src], trip_dst, num_segments=...]
    ppermute x4 -> x0, waiting for transfers between devices: 61 us -> none  [from_behind(): return lax.ppermute(block, axis, route)]
    dot_general x11 -> x0, matrix products: 38.7 us -> none  [the longest x1 6.69 us: edge_pass(): jnp.dot(summed, w_up, preferred_element_type=jnp.float32)]
    all_gather x2 -> x0, waiting for transfers between devices: 22.2 us -> none  [the longest x1 22.2 us: extend(): whole = lax.all_gather(rows, 'gp', axis=0, tiled=True)]
    gather x2 -> x0, local copies, waits for them, and re-layouts: 20.4 us -> none  [the longest x1 11.3 us: edge_back(): atom_grad[targets]]
    reduce_scatter x2 -> x0, waiting for transfers between devices: 13.1 us -> none  [the longest x1 13.1 us: retract(): lax.psum_scatter(shards.reshape(slab_rows, width), 'gp', scatter_dimensio...]
  transfers between devices with their start and end apart: 9 -> 0, of which waited for: 7 -> 0; matrix products, arithmetic and copies ran while one was open for 19% -> 0% of each run, Pallas kernels for 0% -> 0%
where the time goes in v1:
time: 111 us; the launch traced here: 110 us
  Pallas kernels  102 us (92%)
  local copies, waits for them, and re-layouts  6.54 us (6%)
  between operations  1.94 us (2%)
    pallas_call x1, Pallas kernels, per_device(): pl.pallas_call(functools.partial(kernel, dims), out_shape=(jax.ShapeDtype...  100 us
    unnamed x6, local copies, waits for them, and re-layouts  5.76 us

profile of v1, /device:TPU:1, one launch (start us, length us, event | category | flops | bytes accessed | tf_op | source)
XLA Modules:
  0.0 110.2 jit_solution(2070517671177124994)
XLA Ops:
  1.9 1.6 %copy.20.wdown_ref = bf16[512,64]{1,0:T(8,128)(2,1)} copy(bf16[512,64]{0,1:T(8,128)(2,1)} %param.24) | data formatting | bytes 131072 | tf_op args[10]
  3.5 2.0 %copy.19.basis_ref = bf16[2048,64]{1,0:T(8,128)(2,1)} copy(bf16[2048,64]{0,1:T(8,128)(2,1)} %param.20) | data formatting | bytes 524288 | tf_op args[6]
  5.5 100.2 %shard_map.173 = (bf16[32,144,128]{2,1,0:T(8,128)(2,1)}, bf16[256,512]{1,0:T(8,128)(2,1)}) custom-call(s32[1]{0:T(128)S(6)} %copy.22.ecnt_ref, s32[1]{0:T(128)S(6)} %copy.23.tcnt_ref, s32[16,128]{1,0:T(8,128)} %bitcast.4, s32[16,128]{1,0:T(8,128)} %bitcast.5, s32[16,128]{1,0:T(8,128)} %bitcast.6, s32[16,128]{1,0:T(8,128)} %bitcast.7, ...), custom_call_target="tpu_custom_call" | custom-call | tf_op jit(solution)/shard_map/pallas_call | solution.py:425
  105.7 0.0 copy-start
  105.7 1.3 %copy-done = bf16[32,144,128]{2,1,0:T(8,128)(2,1)S(1)} copy-done((bf16[32,144,128]{2,1,0:T(8,128)(2,1)S(1)}, bf16[32,144,128]{2,1,0:T(8,128)(2,1)}, u32[]{:S(2)}) %copy-start) | copy-done | bytes 1179672
  106.9 0.0 copy-start.1
  106.9 0.9 copy-done.1
  107.9 1.6 %shard_map.174 = (bf16[256,512]{1,0:T(8,128)(2,1)}, f32[512,512]{1,0:T(8,128)}, f32[512,64]{1,0:T(8,128)S(1)}, f32[64,512]{1,0:T(8,128)}, f32[512,512]{1,0:T(8,128)}) custom-call(bf16[32,144,128]{2,1,0:T(8,128)(2,1)S(1)} %copy-done, bf16[256,512]{1,0:T(8,128)(2,1)S(1)} %copy-done.1), custom_call_target="tpu_custom_call" | custom-call | tf_op jit(solution)/shard_map/pallas_call | solution.py:457
  109.5 0.8 copy.21
Async XLA Ops:
  105.7 1.3 %copy-start = (bf16[32,144,128]{2,1,0:T(8,128)(2,1)S(1)}, bf16[32,144,128]{2,1,0:T(8,128)(2,1)}, u32[]{:S(2)}) copy-start(bf16[32,144,128]{2,1,0:T(8,128)(2,1)} %get-tuple-element.7.full_ref) | copy-start | bytes 3538948
  106.9 0.9 copy-start.1

commit v2 on v1

v2 whole, which is shorter than its diff:
```python
import functools
import math

import jax
import jax.numpy as jnp
from jax import lax
from jax.experimental import pallas as pl
from jax.experimental.pallas import tpu as pltpu
from jax.sharding import PartitionSpec as P

BF = jnp.bfloat16
F32 = jnp.float32
MESH = pl.DeviceIdType.MESH
GH = 128
OWN = 256
ROWS = 512
SLOTS = 2048
WIDTH = 512
DT = 64
LO = 256
BLK = 512


def dims_of(slabs):
    return {64: (4, 4, 4), 4: (1, 1, 4), 2: (1, 1, 2)}[slabs]


def nn(a, b):
    return lax.dot_general(a, b, (((1,), (0,)), ((), ())), preferred_element_type=F32)


def nt(a, b):
    return lax.dot_general(a, b, (((1,), (1,)), ((), ())), preferred_element_type=F32)


def tn(a, b):
    return lax.dot_general(a, b, (((0,), (0,)), ((), ())), preferred_element_type=F32)


def lanes(shape):
    return lax.broadcasted_iota(jnp.int32, shape, len(shape) - 1)


def pick_columns(index, first, width):
    lane = lanes(index.shape)
    local = index - first
    return jnp.concatenate(
        [jnp.where(local == lane + 128 * j, 1.0, 0.0).astype(BF) for j in range(width // 128)], axis=1
    )


def pick_rows(index, first, height):
    shape = (height, index.shape[1])
    row = lax.broadcasted_iota(jnp.int32, shape, 0)
    return jnp.where(row == jnp.broadcast_to(index - first, shape), 1.0, 0.0).astype(BF)


def table_row(src):
    up = src - 1536
    lower = 4 * OWN + ((src >> 7) << 8) + (src & 127)
    upper = 4 * OWN + ((up >> 7) << 8) + GH + (up & 127)
    return jnp.where(src < 512, lower, jnp.where(src < 1536, src - 512, upper))


def kernel(
    dims,
    ecnt_ref, tcnt_ref, src_ref, dst_ref, tin_ref, tout_ref, wdown_ref, wt_ref,
    atoms_hbm, cot_hbm, msg_hbm, basis_hbm, wa_hbm, wb_hbm,
    full_out, grad_out,
    mid, rim, cots, msg, basis, wa, wb, picked, inc, dpre,
    src_col, dst_col, tin_col, tout_col, rows, basis2, wdown2, wt2,
    down, dn, acc_s, sm,
    dt, rd, ed, re, own_sum, dt2, rd2, ed2, re2, rims_out, rims_in, rims2_out, rims2_in,
    acc_wa, acc_wb, acc_wt, acc_wd, acc_wx, pieces, rc, half, rx, late, rc2, half2, rx2,
    zbuf, rz_main, rz_small, full,
    send, recv, local_sem,
):
    Y, ZH, X = dims
    XY = X * Y
    Z = 2 * ZH
    nb = 16 // XY
    tile = 128 // Z
    dom = lax.axis_index("dom")
    gp = lax.axis_index("gp")
    slabs = Y * ZH * X
    x = lax.rem(dom, X)
    zh = lax.rem(lax.div(dom, X), ZH)
    y = lax.div(dom, X * ZH)
    core = lax.rem(gp, 2)
    zl = lax.div(gp, 2)
    z = zh * 2 + zl

    sib = {"dom": dom, "gp": zl * 2 + (1 - core)}
    zpart = {"dom": dom, "gp": (1 - zl) * 2 + core}
    kz = (1 - zl) * 2 + core
    above = {"dom": lax.rem(dom + 1, slabs), "gp": gp}
    below = {"dom": lax.rem(dom + slabs - 1, slabs), "gp": gp}
    xy_peers = []
    for j in range(1, XY):
        px = lax.rem(x + j // Y, X)
        py = lax.rem(y + j % Y, Y)
        xy_peers.append((px * Y + py, {"dom": (py * ZH + zh) * X + px, "gp": gp}))
    z_peers = []
    for j in range(1, Z):
        pz = lax.rem(z + j, Z)
        z_peers.append((pz, {"dom": (y * ZH + lax.div(pz, 2)) * X + x, "gp": lax.rem(pz, 2) * 2 + core}))

    barrier = pltpu.get_barrier_semaphore()
    others = [sib, above, below] + [d for _, d in xy_peers] + [d for _, d in z_peers]
    for d in others:
        pl.semaphore_signal(barrier, inc=1, device_id=d, device_id_type=MESH)

    count = [0]
    started = []

    def remote(src, dst, device):
        i = count[0]
        count[0] += 1
        c = pltpu.make_async_remote_copy(
            src_ref=src, dst_ref=dst, send_sem=send.at[i], recv_sem=recv.at[i],
            device_id=device, device_id_type=MESH,
        )
        c.start()
        started.append(c)
        return c

    local = []
    for i, (src, dst) in enumerate(
        (
            (atoms_hbm, mid.at[gp]), (cot_hbm, cots.at[gp]), (basis_hbm, basis),
            (wa_hbm, wa), (msg_hbm, msg), (wb_hbm, wb),
        )
    ):
        c = pltpu.make_async_copy(src, dst, local_sem.at[i])
        c.start()
        local.append(c)
    atoms_in, cot_in, basis_in, wa_in, msg_in, wb_in = local

    pl.semaphore_wait(barrier, len(others))

    low = pl.ds(0, GH)
    high = pl.ds(GH, GH)
    to_above = remote(atoms_hbm.at[high], rim.at[gp, low], above)
    to_below = remote(atoms_hbm.at[low], rim.at[gp, high], below)
    to_z = remote(atoms_hbm, mid.at[gp], zpart)
    to_sib = remote(atoms_hbm, mid.at[gp], sib)

    edges = ecnt_ref[0]
    trips = tcnt_ref[0]
    for n, (ref, col) in enumerate(
        ((src_ref, src_col), (dst_ref, dst_col), (tin_ref, tin_col), (tout_ref, tout_col))
    ):
        flat = ref[...]
        if n == 0:
            flat = table_row(flat)
        for j in range(SLOTS // 128):
            line = flat[j : j + 1]
            rows[n : n + 1, 128 * j : 128 * (j + 1)] = line
            col[128 * j : 128 * (j + 1)] = jnp.transpose(jnp.broadcast_to(line, (128, 128)))
    wdown2[...] = jnp.concatenate([wdown_ref[...], wdown_ref[...]], axis=0)
    wt2[...] = jnp.concatenate([wt_ref[...], wt_ref[...]], axis=0)
    basis_in.wait()
    twice = jnp.where(
        lax.broadcasted_iota(jnp.int32, (DT, 128), 0) == (lanes((DT, 128)) & (DT - 1)), 1.0, 0.0
    ).astype(BF)
    valid = lax.broadcasted_iota(jnp.int32, (SLOTS, 128), 0) < trips
    basis2[...] = jnp.where(valid, tn(basis[...], twice), 0.0)

    atoms_in.wait()
    to_sib.wait_recv()
    to_above.wait_recv()
    z_low = remote(rim.at[gp, low], rim.at[gp, low], zpart)
    s_low = remote(rim.at[gp, low], rim.at[gp, low], sib)
    to_below.wait_recv()
    z_high = remote(rim.at[gp, high], rim.at[gp, high], zpart)
    s_high = remote(rim.at[gp, high], rim.at[gp, high], sib)
    z_cot = remote(cot_hbm, cots.at[gp], zpart)
    s_cot = remote(cot_hbm, cots.at[gp], sib)
    to_z.wait_recv()
    f_mid = remote(mid.at[kz], mid.at[kz], sib)
    f_mid.wait_recv()

    def block(b):
        return pl.ds(pl.multiple_of(b * BLK, BLK), BLK)

    def gather(index, first, source):
        got = nn(pick_columns(index, first, OWN), source[0])
        for k in range(1, 4):
            got = got + nn(pick_columns(index, first + k * OWN, OWN), source[k])
        return got

    def edge_own(b, carry):
        picked[block(b)] = gather(src_col[block(b)], 0, mid).astype(BF)
        return carry

    lax.fori_loop(0, SLOTS // BLK, edge_own, 0)

    z_low.wait_recv()
    f_low = remote(rim.at[kz, low], rim.at[kz, low], sib)
    z_high.wait_recv()
    f_high = remote(rim.at[kz, high], rim.at[kz, high], sib)
    for c in (s_low, s_high, f_low, f_high):
        c.wait_recv()
    wa_in.wait()
    msg_in.wait()

    def row_mask(b, width):
        return lax.broadcasted_iota(jnp.int32, (BLK, width), 0) + b * BLK < edges

    def edge_in(b, carry):
        at = block(b)
        got = (picked[at].astype(F32) + gather(src_col[at], 4 * OWN, rim)).astype(BF)
        picked[at] = got
        proj = nn(got, wa[...]).astype(BF).astype(F32)
        value = jnp.where(row_mask(b, WIDTH), proj + msg[at].astype(F32), 0.0)
        inc[at] = value
        down[at] = nt(value.astype(BF), wdown2[...]).astype(BF)
        return carry

    lax.fori_loop(0, SLOTS // BLK, edge_in, 0)
    z_cot.wait_recv()
    f_cot = remote(cots.at[kz], cots.at[kz], sib)

    def pack(source):
        first = lanes((LO, 128)) < DT
        for j in range(4):
            a = source[2 * j * LO : (2 * j + 1) * LO].astype(F32)
            b = source[(2 * j + 1) * LO : (2 * j + 2) * LO].astype(F32)
            dn[:, 128 * j : 128 * (j + 1)] = jnp.where(first, a, b).astype(BF)

    def unpack():
        first = lanes((LO, 128)) < DT
        for j in range(4):
            v = acc_s[:, 128 * j : 128 * (j + 1)]
            sm[2 * j * LO : (2 * j + 1) * LO] = jnp.where(first, v, 0.0).astype(BF)
            sm[(2 * j + 1) * LO : (2 * j + 2) * LO] = jnp.where(first, 0.0, v).astype(BF)

    def triplets(from_col, to_col, to_row):
        half_lane = jnp.where(lanes((BLK, 128)) < DT, 0, 1)
        acc_s[...] = jnp.zeros_like(acc_s)

        def body(b, carry):
            at = block(b)
            frm = from_col[at]
            to = to_col[at]
            got = nn(pick_columns(frm & (LO - 1), 0, LO), dn[...])
            frm_hi = frm >> 8
            to_hi = to >> 8
            value = jnp.where(frm_hi == half_lane, got[:, 0:128], 0.0)
            for j in range(1, 4):
                value = value + jnp.where(
                    frm_hi == half_lane + 2 * j, got[:, 128 * j : 128 * (j + 1)], 0.0
                )
            value = value + pltpu.roll(value, DT, 1)
            value = value * basis2[at]
            spread = jnp.concatenate(
                [jnp.where(to_hi == half_lane + 2 * j, value, 0.0).astype(BF) for j in range(4)], axis=1
            )
            line = rows[to_row : to_row + 1, block(b)]
            acc_s[...] += nn(pick_rows(line & (LO - 1), 0, LO), spread)
            return carry

        lax.fori_loop(0, SLOTS // BLK, body, 0)

    pack(down)
    triplets(tin_col, tout_col, 3)
    unpack()
    cot_in.wait()
    wb_in.wait()
    s_cot.wait_recv()
    f_cot.wait_recv()

    for acc in (acc_wa, acc_wb, acc_wt, acc_wd, acc_wx):
        acc[...] = jnp.zeros_like(acc)

    def edge_mid(b, carry):
        at = block(b)
        mask = row_mask(b, WIDTH)
        cot = gather(dst_col[at], 0, cots).astype(BF)
        atom_grad = nt(cot, wb[...])
        summed = sm[at]
        pre = inc[at] + nn(summed, wt2[...])
        sig = jax.nn.sigmoid(pre)
        out = jnp.where(mask, pre * sig, 0.0).astype(BF)
        grad = jnp.where(mask, atom_grad * sig * (1.0 + pre * (1.0 - sig)), 0.0).astype(BF)
        dpre[at] = grad
        acc_wb[...] += tn(out, cot)
        acc_wa[...] += tn(picked[at], grad)
        acc_wt[...] += tn(summed, grad)
        down[at] = nt(grad, wt2[...]).astype(BF)
        return carry

    lax.fori_loop(0, SLOTS // BLK, edge_mid, 0)

    def fold(acc, r, cols):
        return (acc[16 * r : 16 * (r + 1), cols] + acc[DT + 16 * r : DT + 16 * (r + 1), cols]).astype(BF)

    for s in range(32):
        r, c = (s % 16) // 4, s % 4
        cols = slice(128 * c, 128 * (c + 1))
        pieces[s, 0:128] = (acc_wa if s < 16 else acc_wb)[128 * r : 128 * (r + 1), cols].astype(BF)
        pieces[s, 128:144] = fold(acc_wt, r, cols) if s < 16 else jnp.zeros((16, 128), BF)
    not_mine = pl.ds((1 - core) * 16, 16)
    mine = pl.ds(core * 16, 16)
    w_core = remote(pieces.at[not_mine], rc, sib)

    def table_grad(owner, source, out, who):
        for part in range(2):
            first = (4 + owner) * OWN if part == 0 else owner * OWN
            total = None
            for b in range(SLOTS // BLK):
                cols = slice(BLK * b, BLK * (b + 1))
                line = rows[0:1, cols]
                choice = jnp.concatenate(
                    [pick_rows(line, first, OWN), pick_rows(line, first + 2 * OWN, OWN)], axis=0
                )
                term = nn(choice, source[cols])
                total = term if total is None else total + term
            total = total.astype(BF)
            out[who, 0, OWN * part : OWN * (part + 1)] = total[0:OWN]
            out[who, 1, OWN * part : OWN * (part + 1)] = total[OWN:]

    table_grad(1 - core, dpre, dt, 0)
    d_core = remote(dt.at[0], rd, sib)
    w_core.wait_recv()
    half[...] = (pieces[mine].astype(F32) + rc[...].astype(F32)).astype(BF)
    w_xy = [
        remote(half.at[pl.ds(s * nb, nb)], rx.at[j], d) for j, (s, d) in enumerate(xy_peers)
    ]
    table_grad(core, dpre, dt, 1)
    d_core.wait_recv()
    ed[...] = (dt[1, 1 - zl].astype(F32) + rd[1 - zl].astype(F32)).astype(BF)
    rim_part = pl.ds(0, OWN)
    mid_part = pl.ds(OWN, OWN)
    d_rim = remote(ed.at[rim_part], re.at[rim_part], zpart)
    d_mid = remote(ed.at[mid_part], re.at[mid_part], zpart)

    pack(down)
    triplets(tout_col, tin_col, 2)
    unpack()

    def edge_out(b, carry):
        at = block(b)
        back = jnp.where(row_mask(b, 128), sm[at].astype(F32), 0.0).astype(BF)
        sm[at] = back
        acc_wd[...] += tn(back, inc[at].astype(BF))
        acc_wx[...] += tn(back, picked[at])
        return carry

    lax.fori_loop(0, SLOTS // BLK, edge_out, 0)
    for s in range(32):
        r, c = (s % 16) // 4, s % 4
        late[s] = fold(acc_wd if s < 16 else acc_wx, r, slice(128 * c, 128 * (c + 1)))
    l_core = remote(late.at[not_mine], rc2, sib)
    table_grad(1 - core, sm, dt2, 0)
    d2_core = remote(dt2.at[0], rd2, sib)
    l_core.wait_recv()
    half2[...] = (late[mine].astype(F32) + rc2[...].astype(F32)).astype(BF)
    l_xy = [
        remote(half2.at[pl.ds(s * nb, nb)], rx2.at[j], d) for j, (s, d) in enumerate(xy_peers)
    ]

    own_s = x * Y + y
    own_rows = pl.ds(pl.multiple_of(z * tile, tile), tile)
    own_piece = pl.ds(core * 16 + own_s * nb, nb)

    def sum_xy(copies, buffer, received):
        for c in copies:
            c.wait_recv()
        total = buffer[pl.ds(own_s * nb, nb)].astype(F32)
        for j in range(XY - 1):
            total = total + received[j].astype(F32)
        return total.astype(BF)

    zbuf[:, 0:144] = sum_xy(w_xy, half, rx)
    w_z = []
    for j, (pz, d) in enumerate(z_peers):
        part = pl.ds(pl.multiple_of(pz * tile, tile), tile)
        w_z.append(remote(zbuf.at[:, part], rz_main.at[j + 1], d))

    table_grad(core, sm, dt2, 1)
    d2_core.wait_recv()
    ed2[...] = (dt2[1, 1 - zl].astype(F32) + rd2[1 - zl].astype(F32)).astype(BF)
    d2_z = remote(ed2, re2, zpart)

    zbuf[:, 144:160] = sum_xy(l_xy, half2, rx2)
    l_z = [
        remote(zbuf.at[:, pl.ds(128, 32)], rz_small.at[j + 1], d) for j, (_, d) in enumerate(z_peers)
    ]
    rz_small[0] = zbuf[:, 128:160]

    d_rim.wait_recv()
    own_sum[rim_part] = dt[1, zl, rim_part].astype(F32) + rd[zl, rim_part].astype(F32) + re[rim_part].astype(F32)
    rims_out[...] = own_sum[rim_part].astype(BF)
    to_tails = remote(rims_out.at[low], rims_in.at[0], below)
    to_heads = remote(rims_out.at[high], rims_in.at[1], above)

    for c in w_z:
        c.wait_recv()
    total = zbuf[:, own_rows].astype(F32)
    for j in range(1, Z):
        total = total + rz_main[j].astype(F32)
    full[own_piece, own_rows] = total.astype(BF)
    g_z = [
        remote(full.at[own_piece, own_rows], full.at[own_piece, own_rows], d) for _, d in z_peers
    ]
    for c in l_z:
        c.wait_recv()
    small = rz_small[lax.rem(Z - z, Z)].astype(F32)
    for j in range(1, Z):
        small = small + rz_small[lax.rem(j + Z - z, Z)].astype(F32)
    full[own_piece, 128:160] = small.astype(BF)
    for c in g_z:
        c.wait_recv()
    g_xy = [remote(full.at[own_piece], full.at[own_piece], d) for _, d in xy_peers]

    d2_z.wait_recv()
    sum2 = dt2[1, zl].astype(F32) + rd2[zl].astype(F32) + re2[...].astype(F32)
    rims2_out[...] = sum2[0:OWN].astype(BF)
    to_tails2 = remote(rims2_out.at[low], rims2_in.at[0], below)
    to_heads2 = remote(rims2_out.at[high], rims2_in.at[1], above)
    d_mid.wait_recv()
    own_sum[mid_part] = dt[1, zl, mid_part].astype(F32) + rd[zl, mid_part].astype(F32) + re[mid_part].astype(F32)
    for c in (to_tails, to_heads, to_tails2, to_heads2):
        c.wait_recv()
    narrow = sum2[OWN:] + jnp.concatenate([rims2_in[1].astype(F32), rims2_in[0].astype(F32)], axis=0)
    dproj = own_sum[mid_part] + jnp.concatenate([rims_in[1].astype(F32), rims_in[0].astype(F32)], axis=0)
    dproj = dproj + nn(narrow.astype(BF), wdown2[...])
    coarse = dproj.astype(BF)
    fine = (dproj - coarse.astype(F32)).astype(BF)
    grad_out[...] = (nt(coarse, wa[...]) + nt(fine, wa[...])).astype(BF)

    for c in g_xy:
        c.wait_recv()
    g_core = remote(full.at[mine], full.at[mine], sib)
    g_core.wait_recv()
    full_out[...] = full[...]
    for c in started:
        c.wait_send()


def finish(factor, grad_hbm, full_ref, wdown_ref, gatoms_hbm, gwa_ref, gwd_ref, gwt_ref, gwb_ref, sem):
    through = pltpu.make_async_copy(grad_hbm, gatoms_hbm, sem.at[0])
    through.start()

    def rows_of(first, part):
        return jnp.concatenate(
            [
                jnp.concatenate([full_ref[first + 4 * r + c, part] for c in range(4)], axis=1)
                for r in range(4)
            ],
            axis=0,
        )

    gwt_ref[...] = rows_of(0, slice(128, 144)).astype(F32) * factor
    gwd_ref[...] = rows_of(0, slice(144, 160)).astype(F32) * factor
    gwb_ref[...] = rows_of(16, slice(0, 128)).astype(F32) * factor
    back = tn(rows_of(16, slice(144, 160)), wdown_ref[...])
    gwa_ref[...] = (rows_of(0, slice(0, 128)).astype(F32) + back) * factor
    through.wait()


def per_device(
    slabs, groups,
    atoms, messages, edge_src, edge_dst, trip_in, trip_out, trip_basis, edge_count, trip_count,
    w_a, w_down, w_t, w_b, cotangent,
):
    dims = dims_of(slabs)
    Y, ZH, X = dims
    XY, Z = X * Y, 2 * ZH
    nb, tile = 16 // XY, 128 // Z
    transfers = 32 + 3 * (XY - 1) + 3 * (Z - 1)
    vmem = pl.BlockSpec(memory_space=pltpu.VMEM)
    smem = pl.BlockSpec(memory_space=pltpu.SMEM)
    hbm = pl.BlockSpec(memory_space=pl.ANY)
    index = [a.reshape(16, 128) for a in (edge_src, edge_dst, trip_in, trip_out)]
    w_down = w_down.T
    V = pltpu.VMEM
    full, grad = pl.pallas_call(
        functools.partial(kernel, dims),
        out_shape=(
            jax.ShapeDtypeStruct((32, 160, 128), BF),
            jax.ShapeDtypeStruct((OWN, WIDTH), BF),
        ),
        in_specs=[smem, smem] + [vmem] * 6 + [hbm] * 6,
        out_specs=(vmem, vmem),
        scratch_shapes=[
            V((4, OWN, WIDTH), BF), V((4, OWN, WIDTH), BF), V((4, OWN, WIDTH), BF),
            V((SLOTS, WIDTH), BF), V((DT, SLOTS), BF), V((512, WIDTH), BF), V((512, WIDTH), BF),
            V((SLOTS, WIDTH), BF), V((SLOTS, WIDTH), F32), V((SLOTS, WIDTH), BF),
            V((SLOTS, 128), jnp.int32), V((SLOTS, 128), jnp.int32),
            V((SLOTS, 128), jnp.int32), V((SLOTS, 128), jnp.int32),
            V((8, SLOTS), jnp.int32), V((SLOTS, 128), F32), V((128, WIDTH), BF), V((128, WIDTH), BF),
            V((SLOTS, 128), BF), V((LO, WIDTH), BF), V((LO, WIDTH), F32), V((SLOTS, 128), BF),
            V((2, 2, ROWS, WIDTH), BF), V((2, ROWS, WIDTH), BF), V((ROWS, WIDTH), BF), V((ROWS, WIDTH), BF),
            V((ROWS, WIDTH), F32),
            V((2, 2, ROWS, 128), BF), V((2, ROWS, 128), BF), V((ROWS, 128), BF), V((ROWS, 128), BF),
            V((OWN, WIDTH), BF), V((2, GH, WIDTH), BF), V((OWN, 128), BF), V((2, GH, 128), BF),
            V((512, WIDTH), F32), V((512, WIDTH), F32), V((128, WIDTH), F32), V((128, WIDTH), F32),
            V((128, WIDTH), F32),
            V((32, 144, 128), BF), V((16, 144, 128), BF), V((16, 144, 128), BF),
            V((XY - 1, nb, 144, 128), BF),
            V((32, 16, 128), BF), V((16, 16, 128), BF), V((16, 16, 128), BF), V((XY - 1, nb, 16, 128), BF),
            V((nb, 160, 128), BF), V((Z, nb, tile, 128), BF), V((Z, nb, 32, 128), BF), V((32, 160, 128), BF),
            pltpu.SemaphoreType.DMA((transfers,)), pltpu.SemaphoreType.DMA((transfers,)),
            pltpu.SemaphoreType.DMA((6,)),
        ],
        compiler_params=pltpu.CompilerParams(
            collective_id=0, has_side_effects=True, vmem_limit_bytes=60 * 1024 * 1024
        ),
    )(
        edge_count, trip_count, *index, w_down, w_t,
        atoms, cotangent, messages, trip_basis.T, w_a, w_b,
    )
    factor = 1.0 / math.sqrt(OWN * groups * slabs)
    grad, gwa, gwd, gwt, gwb = pl.pallas_call(
        functools.partial(finish, factor),
        out_shape=(
            jax.ShapeDtypeStruct((OWN, WIDTH), BF),
            jax.ShapeDtypeStruct((512, WIDTH), F32),
            jax.ShapeDtypeStruct((DT, WIDTH), F32),
            jax.ShapeDtypeStruct((DT, WIDTH), F32),
            jax.ShapeDtypeStruct((512, WIDTH), F32),
        ),
        in_specs=[hbm, vmem, vmem],
        out_specs=(hbm, vmem, vmem, vmem, vmem),
        scratch_shapes=[pltpu.SemaphoreType.DMA((1,))],
        compiler_params=pltpu.CompilerParams(vmem_limit_bytes=32 * 1024 * 1024),
    )(grad, full, w_down)
    return grad, gwa, gwd.T, gwt, gwb


def solution(mesh):
    both = P(("dom", "gp"))
    rows = P(("dom", "gp"), None)
    in_specs = (rows, rows, both, both, both, both, rows, both, both, P(), P(), P(), P(), rows)
    out_specs = (rows, P(), P(), P(), P())
    return jax.shard_map(
        functools.partial(per_device, mesh.shape["dom"], mesh.shape["gp"]),
        mesh=mesh, in_specs=in_specs, out_specs=out_specs, check_vma=False,
    )
```

time: 111 us -> 99.5 us (0.90)
  Pallas kernels: 102 us -> 93.8 us
  local copies, waits for them, and re-layouts: 6.54 us -> 2.26 us
    pallas_call x1, Pallas kernels: 100 us -> 91.5 us  [per_device(): pl.pallas_call(functools.partial(kernel, dims), out_shape=(jax.ShapeDtype...]
    unnamed x6, local copies, waits for them, and re-layouts: 5.76 us -> 2.26 us
where the time goes in v2:
time: 99.5 us; the launch traced here: 98.2 us
  Pallas kernels  93.8 us (94%)
  local copies, waits for them, and re-layouts  2.26 us (2%)
  between operations  2.15 us (2%)
    pallas_call x1, Pallas kernels, per_device(): pl.pallas_call(functools.partial(kernel, dims), out_shape=(jax.ShapeDtype...  91.5 us
    pallas_call x1, Pallas kernels, per_device(): pl.pallas_call(functools.partial(finish, factor), out_shape=(jax.ShapeDty...  2.28 us
    unnamed x6, local copies, waits for them, and re-layouts  2.26 us

profile of v2, /device:TPU:1, one launch (start us, length us, event | category | flops | bytes accessed | tf_op | source)
XLA Modules:
  0.0 98.2 jit_solution(18339571345010514588)
XLA Ops:
  0.6 0.0 copy-start.1
  2.0 91.5 %shard_map.173 = (bf16[32,160,128]{2,1,0:T(8,128)(2,1)}, bf16[256,512]{1,0:T(8,128)(2,1)}) custom-call(s32[1]{0:T(128)S(6)} %copy.19.ecnt_ref, s32[1]{0:T(128)S(6)} %copy.20.tcnt_ref, s32[16,128]{1,0:T(8,128)} %bitcast.10, s32[16,128]{1,0:T(8,128)} %bitcast.11, s32[16,128]{1,0:T(8,128)} %bitcast.12, s32[16,128]{1,0:T(8,128)} %bitcast.13, ...), custom_call_target="tpu_custom_call" | custom-call | tf_op jit(solution)/shard_map/pallas_call | solution.py:479
  93.5 0.0 copy-done.1
  93.5 0.0 copy-start
  93.5 1.3 %copy-done = bf16[32,160,128]{2,1,0:T(8,128)(2,1)S(1)} copy-done((bf16[32,160,128]{2,1,0:T(8,128)(2,1)S(1)}, bf16[32,160,128]{2,1,0:T(8,128)(2,1)}, u32[]{:S(2)}) %copy-start) | copy-done | bytes 1310744
  94.8 0.0 copy-start.2
  94.8 0.9 copy-done.2
  95.8 2.3 %shard_map.174 = (bf16[256,512]{1,0:T(8,128)(2,1)}, f32[512,512]{1,0:T(8,128)}, f32[64,512]{1,0:T(8,128)}, f32[64,512]{1,0:T(8,128)}, f32[512,512]{1,0:T(8,128)}) custom-call(bf16[256,512]{1,0:T(8,128)(2,1)S(1)} %copy-done.2, bf16[32,160,128]{2,1,0:T(8,128)(2,1)S(1)} %copy-done, bf16[64,512]{1,0:T(8,128)(2,1)S(1)} %bitcast.8), custom_call_target="tpu_custom_call" | custom-call | tf_op jit(solution)/shard_map/pallas_call | solution.py:516
Async XLA Ops:
  0.6 92.9 %copy-start.1 = (bf16[512,64]{0,1:T(8,128)(2,1)S(1)}, bf16[512,64]{0,1:T(8,128)(2,1)}, u32[]{:S(2)}) copy-start(bf16[512,64]{0,1:T(8,128)(2,1)} %param.24) | copy-start | bytes 196612
  93.5 1.3 %copy-start = (bf16[32,160,128]{2,1,0:T(8,128)(2,1)S(1)}, bf16[32,160,128]{2,1,0:T(8,128)(2,1)}, u32[]{:S(2)}) copy-start(bf16[32,160,128]{2,1,0:T(8,128)(2,1)} %get-tuple-element.13.full_ref) | copy-start | bytes 3932164
  94.8 0.9 copy-start.2

commit v3 on v2

--- a/solution.py
+++ b/solution.py
@@ -70,7 +70,7 @@
     mid, rim, cots, msg, basis, wa, wb, picked, inc, dpre,
     src_col, dst_col, tin_col, tout_col, rows, basis2, wdown2, wt2,
     down, dn, acc_s, sm,
-    dt, rd, ed, re, own_sum, dt2, rd2, ed2, re2, rims_out, rims_in, rims2_out, rims2_in,
+    dt, rd, ed, re, grad, dt2, rd2, ed2, re2, rims_out, rims_in, rims2_out, rims2_in,
     acc_wa, acc_wb, acc_wt, acc_wd, acc_wx, pieces, rc, half, rx, late, rc2, half2, rx2,
     zbuf, rz_main, rz_small, full,
     send, recv, local_sem,
@@ -145,8 +145,8 @@
     to_z = remote(atoms_hbm, mid.at[gp], zpart)
     to_sib = remote(atoms_hbm, mid.at[gp], sib)
 
-    edges = ecnt_ref[0]
-    trips = tcnt_ref[0]
+    edges = ecnt_ref[...]
+    trips = tcnt_ref[...]
     for n, (ref, col) in enumerate(
         ((src_ref, src_col), (dst_ref, dst_col), (tin_ref, tin_col), (tout_ref, tout_col))
     ):
@@ -163,7 +163,7 @@
     twice = jnp.where(
         lax.broadcasted_iota(jnp.int32, (DT, 128), 0) == (lanes((DT, 128)) & (DT - 1)), 1.0, 0.0
     ).astype(BF)
-    valid = lax.broadcasted_iota(jnp.int32, (SLOTS, 128), 0) < trips
+    valid = lax.broadcasted_iota(jnp.int32, (SLOTS, 128), 0) < jnp.broadcast_to(trips, (SLOTS, 128))
     basis2[...] = jnp.where(valid, tn(basis[...], twice), 0.0)
 
     atoms_in.wait()
@@ -205,7 +205,8 @@
     msg_in.wait()
 
     def row_mask(b, width):
-        return lax.broadcasted_iota(jnp.int32, (BLK, width), 0) + b * BLK < edges
+        shape = (BLK, width)
+        return lax.broadcasted_iota(jnp.int32, shape, 0) < jnp.broadcast_to(edges - b * BLK, shape)
 
     def edge_in(b, carry):
         at = block(b)
@@ -333,7 +334,6 @@
     rim_part = pl.ds(0, OWN)
     mid_part = pl.ds(OWN, OWN)
     d_rim = remote(ed.at[rim_part], re.at[rim_part], zpart)
-    d_mid = remote(ed.at[mid_part], re.at[mid_part], zpart)
 
     pack(down)
     triplets(tout_col, tin_col, 2)
@@ -377,23 +377,17 @@
     for j, (pz, d) in enumerate(z_peers):
         part = pl.ds(pl.multiple_of(pz * tile, tile), tile)
         w_z.append(remote(zbuf.at[:, part], rz_main.at[j + 1], d))
+    d_mid = remote(ed.at[mid_part], re.at[mid_part], zpart)
 
     table_grad(core, sm, dt2, 1)
-    d2_core.wait_recv()
-    ed2[...] = (dt2[1, 1 - zl].astype(F32) + rd2[1 - zl].astype(F32)).astype(BF)
-    d2_z = remote(ed2, re2, zpart)
-
     zbuf[:, 144:160] = sum_xy(l_xy, half2, rx2)
     l_z = [
         remote(zbuf.at[:, pl.ds(128, 32)], rz_small.at[j + 1], d) for j, (_, d) in enumerate(z_peers)
     ]
     rz_small[0] = zbuf[:, 128:160]
-
-    d_rim.wait_recv()
-    own_sum[rim_part] = dt[1, zl, rim_part].astype(F32) + rd[zl, rim_part].astype(F32) + re[rim_part].astype(F32)
-    rims_out[...] = own_sum[rim_part].astype(BF)
-    to_tails = remote(rims_out.at[low], rims_in.at[0], below)
-    to_heads = remote(rims_out.at[high], rims_in.at[1], above)
+    d2_core.wait_recv()
+    ed2[...] = (dt2[1, 1 - zl].astype(F32) + rd2[1 - zl].astype(F32)).astype(BF)
+    d2_z = remote(ed2, re2, zpart)
 
     for c in w_z:
         c.wait_recv()
@@ -404,6 +398,14 @@
     g_z = [
         remote(full.at[own_piece, own_rows], full.at[own_piece, own_rows], d) for _, d in z_peers
     ]
+
+    d_rim.wait_recv()
+    rims_out[...] = (
+        dt[1, zl, rim_part].astype(F32) + rd[zl, rim_part].astype(F32) + re[rim_part].astype(F32)
+    ).astype(BF)
+    to_tails = remote(rims_out.at[low], rims_in.at[0], below)
+    to_heads = remote(rims_out.at[high], rims_in.at[1], above)
+
     for c in l_z:
         c.wait_recv()
     small = rz_small[lax.rem(Z - z, Z)].astype(F32)
@@ -413,51 +415,82 @@
     for c in g_z:
         c.wait_recv()
     g_xy = [remote(full.at[own_piece], full.at[own_piece], d) for _, d in xy_peers]
+    g_core = [remote(full.at[own_piece], full.at[own_piece], sib)]
 
     d2_z.wait_recv()
     sum2 = dt2[1, zl].astype(F32) + rd2[zl].astype(F32) + re2[...].astype(F32)
     rims2_out[...] = sum2[0:OWN].astype(BF)
     to_tails2 = remote(rims2_out.at[low], rims2_in.at[0], below)
     to_heads2 = remote(rims2_out.at[high], rims2_in.at[1], above)
+
+    for j, c in enumerate(g_xy):
+        c.wait_recv()
+        px = lax.rem(x + X - (j + 1) // Y, X)
+        py = lax.rem(y + Y - (j + 1) % Y, Y)
+        piece = pl.ds(core * 16 + (px * Y + py) * nb, nb)
+        g_core.append(remote(full.at[piece], full.at[piece], sib))
+
     d_mid.wait_recv()
-    own_sum[mid_part] = dt[1, zl, mid_part].astype(F32) + rd[zl, mid_part].astype(F32) + re[mid_part].astype(F32)
     for c in (to_tails, to_heads, to_tails2, to_heads2):
         c.wait_recv()
     narrow = sum2[OWN:] + jnp.concatenate([rims2_in[1].astype(F32), rims2_in[0].astype(F32)], axis=0)
-    dproj = own_sum[mid_part] + jnp.concatenate([rims_in[1].astype(F32), rims_in[0].astype(F32)], axis=0)
+    dproj = dt[1, zl, mid_part].astype(F32) + rd[zl, mid_part].astype(F32) + re[mid_part].astype(F32)
+    dproj = dproj + jnp.concatenate([rims_in[1].astype(F32), rims_in[0].astype(F32)], axis=0)
     dproj = dproj + nn(narrow.astype(BF), wdown2[...])
     coarse = dproj.astype(BF)
     fine = (dproj - coarse.astype(F32)).astype(BF)
-    grad_out[...] = (nt(coarse, wa[...]) + nt(fine, wa[...])).astype(BF)
-
-    for c in g_xy:
-        c.wait_recv()
-    g_core = remote(full.at[mine], full.at[mine], sib)
-    g_core.wait_recv()
-    full_out[...] = full[...]
+    grad[...] = (nt(coarse, wa[...]) + nt(fine, wa[...])).astype(BF)
+    grad_copy = pltpu.make_async_copy(grad, grad_out, local_sem.at[6])
+    grad_copy.start()
+
+    for c in g_core:
+        c.wait_recv()
+    full_copy = pltpu.make_async_copy(full, full_out, local_sem.at[7])
+    full_copy.start()
     for c in started:
         c.wait_send()
-
-
-def finish(factor, grad_hbm, full_ref, wdown_ref, gatoms_hbm, gwa_ref, gwd_ref, gwt_ref, gwb_ref, sem):
-    through = pltpu.make_async_copy(grad_hbm, gatoms_hbm, sem.at[0])
-    through.start()
+    grad_copy.wait()
+    full_copy.wait()
+
+
+def finish(
+    factor, grad_hbm, full_hbm, wdown_ref, gatoms_hbm, gwa_hbm, gwd_hbm, gwt_hbm, gwb_hbm,
+    full, gwa, gwd, gwt, gwb, sem,
+):
+    copies = []
+
+    def copy(src, dst):
+        c = pltpu.make_async_copy(src, dst, sem.at[len(copies)])
+        c.start()
+        copies.append(c)
+        return c
+
+    second = copy(full_hbm.at[pl.ds(16, 16)], full.at[pl.ds(16, 16)])
+    first = copy(full_hbm.at[pl.ds(0, 16)], full.at[pl.ds(0, 16)])
+    copy(grad_hbm, gatoms_hbm)
 
     def rows_of(first, part):
         return jnp.concatenate(
             [
-                jnp.concatenate([full_ref[first + 4 * r + c, part] for c in range(4)], axis=1)
+                jnp.concatenate([full[first + 4 * r + c, part] for c in range(4)], axis=1)
                 for r in range(4)
             ],
             axis=0,
         )
 
-    gwt_ref[...] = rows_of(0, slice(128, 144)).astype(F32) * factor
-    gwd_ref[...] = rows_of(0, slice(144, 160)).astype(F32) * factor
-    gwb_ref[...] = rows_of(16, slice(0, 128)).astype(F32) * factor
+    second.wait()
+    gwb[...] = rows_of(16, slice(0, 128)).astype(F32) * factor
+    copy(gwb, gwb_hbm)
     back = tn(rows_of(16, slice(144, 160)), wdown_ref[...])
-    gwa_ref[...] = (rows_of(0, slice(0, 128)).astype(F32) + back) * factor
-    through.wait()
+    first.wait()
+    gwa[...] = (rows_of(0, slice(0, 128)).astype(F32) + back) * factor
+    copy(gwa, gwa_hbm)
+    gwt[...] = rows_of(0, slice(128, 144)).astype(F32) * factor
+    copy(gwt, gwt_hbm)
+    gwd[...] = rows_of(0, slice(144, 160)).astype(F32) * factor
+    copy(gwd, gwd_hbm)
+    for c in copies[2:]:
+        c.wait()
 
 
 def per_device(
@@ -469,9 +502,8 @@
     Y, ZH, X = dims
     XY, Z = X * Y, 2 * ZH
     nb, tile = 16 // XY, 128 // Z
-    transfers = 32 + 3 * (XY - 1) + 3 * (Z - 1)
+    transfers = 32 + 4 * (XY - 1) + 3 * (Z - 1)
     vmem = pl.BlockSpec(memory_space=pltpu.VMEM)
-    smem = pl.BlockSpec(memory_space=pltpu.SMEM)
     hbm = pl.BlockSpec(memory_space=pl.ANY)
     index = [a.reshape(16, 128) for a in (edge_src, edge_dst, trip_in, trip_out)]
     w_down = w_down.T
@@ -482,8 +514,8 @@
             jax.ShapeDtypeStruct((32, 160, 128), BF),
             jax.ShapeDtypeStruct((OWN, WIDTH), BF),
         ),
-        in_specs=[smem, smem] + [vmem] * 6 + [hbm] * 6,
-        out_specs=(vmem, vmem),
+        in_specs=[vmem] * 8 + [hbm] * 6,
+        out_specs=(hbm, hbm),
         scratch_shapes=[
             V((4, OWN, WIDTH), BF), V((4, OWN, WIDTH), BF), V((4, OWN, WIDTH), BF),
             V((SLOTS, WIDTH), BF), V((DT, SLOTS), BF), V((512, WIDTH), BF), V((512, WIDTH), BF),
@@ -493,7 +525,7 @@
             V((8, SLOTS), jnp.int32), V((SLOTS, 128), F32), V((128, WIDTH), BF), V((128, WIDTH), BF),
             V((SLOTS, 128), BF), V((LO, WIDTH), BF), V((LO, WIDTH), F32), V((SLOTS, 128), BF),
             V((2, 2, ROWS, WIDTH), BF), V((2, ROWS, WIDTH), BF), V((ROWS, WIDTH), BF), V((ROWS, WIDTH), BF),
-            V((ROWS, WIDTH), F32),
+            V((OWN, WIDTH), BF),
             V((2, 2, ROWS, 128), BF), V((2, ROWS, 128), BF), V((ROWS, 128), BF), V((ROWS, 128), BF),
             V((OWN, WIDTH), BF), V((2, GH, WIDTH), BF), V((OWN, 128), BF), V((2, GH, 128), BF),
             V((512, WIDTH), F32), V((512, WIDTH), F32), V((128, WIDTH), F32), V((128, WIDTH), F32),
@@ -503,13 +535,13 @@
             V((32, 16, 128), BF), V((16, 16, 128), BF), V((16, 16, 128), BF), V((XY - 1, nb, 16, 128), BF),
             V((nb, 160, 128), BF), V((Z, nb, tile, 128), BF), V((Z, nb, 32, 128), BF), V((32, 160, 128), BF),
             pltpu.SemaphoreType.DMA((transfers,)), pltpu.SemaphoreType.DMA((transfers,)),
-            pltpu.SemaphoreType.DMA((6,)),
+            pltpu.SemaphoreType.DMA((8,)),
         ],
         compiler_params=pltpu.CompilerParams(
             collective_id=0, has_side_effects=True, vmem_limit_bytes=60 * 1024 * 1024
         ),
     )(
-        edge_count, trip_count, *index, w_down, w_t,
+        edge_count.reshape(1, 1), trip_count.reshape(1, 1), *index, w_down, w_t,
         atoms, cotangent, messages, trip_basis.T, w_a, w_b,
     )
     factor = 1.0 / math.sqrt(OWN * groups * slabs)
@@ -522,10 +554,13 @@
             jax.ShapeDtypeStruct((DT, WIDTH), F32),
             jax.ShapeDtypeStruct((512, WIDTH), F32),
         ),
-        in_specs=[hbm, vmem, vmem],
-        out_specs=(hbm, vmem, vmem, vmem, vmem),
-        scratch_shapes=[pltpu.SemaphoreType.DMA((1,))],
-        compiler_params=pltpu.CompilerParams(vmem_limit_bytes=32 * 1024 * 1024),
+        in_specs=[hbm, hbm, vmem],
+        out_specs=(hbm,) * 5,
+        scratch_shapes=[
+            V((32, 160, 128), BF), V((512, WIDTH), F32), V((DT, WIDTH), F32), V((DT, WIDTH), F32),
+            V((512, WIDTH), F32), pltpu.SemaphoreType.DMA((8,)),
+        ],
+        compiler_params=pltpu.CompilerParams(vmem_limit_bytes=60 * 1024 * 1024),
     )(grad, full, w_down)
     return grad, gwa, gwd.T, gwt, gwb
 

time: 99.5 us -> 107 us (1.075)
  Pallas kernels: 93.8 us -> 105 us
  local copies, waits for them, and re-layouts: 2.26 us -> 0 us
    pallas_call x1, Pallas kernels: 2.28 us -> 9.96 us  [per_device(): pl.pallas_call(functools.partial(finish, factor), out_shape=(jax.ShapeDty...]
    pallas_call x1, Pallas kernels: 91.5 us -> 94.7 us  [per_device(): pl.pallas_call(functools.partial(kernel, dims), out_shape=(jax.ShapeDtype...]
    unnamed x6 -> x0, local copies, waits for them, and re-layouts: 2.26 us -> none
where the time goes in v3:
time: 107 us
  Pallas kernels  105 us (98%)
  between operations  2.09 us (2%)
    pallas_call x1, Pallas kernels, per_device(): pl.pallas_call(functools.partial(kernel, dims), out_shape=(jax.ShapeDtype...  94.7 us
    pallas_call x1, Pallas kernels, per_device(): pl.pallas_call(functools.partial(finish, factor), out_shape=(jax.ShapeDty...  9.96 us

profile of v3, /device:TPU:1, one launch (start us, length us, event | category | flops | bytes accessed | tf_op | source)
XLA Modules:
  0.0 106.7 jit_solution(9178342633073493438)
XLA Ops:
  1.9 94.7 %shard_map.173 = (bf16[32,160,128]{2,1,0:T(8,128)(2,1)}, bf16[256,512]{1,0:T(8,128)(2,1)}) custom-call(s32[1,1]{1,0:T(1,128)} %bitcast.9.ecnt_ref, s32[1,1]{1,0:T(1,128)} %bitcast.10.tcnt_ref, s32[16,128]{1,0:T(8,128)} %bitcast.14, s32[16,128]{1,0:T(8,128)} %bitcast.15, s32[16,128]{1,0:T(8,128)} %bitcast.16, s32[16,128]{1,0:T(8,128)} %bitcast.17, ...), custom_call_target="tpu_custom_call" | custom-call | tf_op jit(solution)/shard_map/pallas_call | solution.py:511
  96.6 10.0 %shard_map.174 = (bf16[256,512]{1,0:T(8,128)(2,1)}, f32[512,512]{1,0:T(8,128)}, f32[64,512]{1,0:T(8,128)}, f32[64,512]{1,0:T(8,128)}, f32[512,512]{1,0:T(8,128)}) custom-call(bf16[256,512]{1,0:T(8,128)(2,1)} %get-tuple-element.12.grad_hbm, bf16[32,160,128]{2,1,0:T(8,128)(2,1)} %get-tuple-element.13.full_hbm, bf16[64,512]{1,0:T(8,128)(2,1)} %bitcast.12), custom_call_target="tpu_custom_call" | custom-call | tf_op jit(solution)/shard_map/pallas_call | solution.py:548

commit v4 on v3

--- a/solution.py
+++ b/solution.py
@@ -66,20 +66,22 @@
     dims,
     ecnt_ref, tcnt_ref, src_ref, dst_ref, tin_ref, tout_ref, wdown_ref, wt_ref,
     atoms_hbm, cot_hbm, msg_hbm, basis_hbm, wa_hbm, wb_hbm,
-    full_out, grad_out,
+    full_a_out, full_b_out, grad_out,
     mid, rim, cots, msg, basis, wa, wb, picked, inc, dpre,
     src_col, dst_col, tin_col, tout_col, rows, basis2, wdown2, wt2,
     down, dn, acc_s, sm,
     dt, rd, ed, re, grad, dt2, rd2, ed2, re2, rims_out, rims_in, rims2_out, rims2_in,
-    acc_wa, acc_wb, acc_wt, acc_wd, acc_wx, pieces, rc, half, rx, late, rc2, half2, rx2,
-    zbuf, rz_main, rz_small, full,
+    acc_wa, acc_wb, acc_wt, acc_wd, acc_wx, picked_cot, slope,
+    pieces_b, rc_b, half_b, rx_b, z_b, rz_b, fz_b, full_b,
+    pieces_a, rc_a, half_a, rx_a, z_a, rz_a, fz_a, full_a,
+    late, rc_l, half_l, rx_l, small_z, rz_small,
     send, recv, local_sem,
 ):
     Y, ZH, X = dims
     XY = X * Y
     Z = 2 * ZH
     nb = 16 // XY
-    tile = 128 // Z
+    tile = 64 // Z
     dom = lax.axis_index("dom")
     gp = lax.axis_index("gp")
     slabs = Y * ZH * X
@@ -274,36 +276,94 @@
     for acc in (acc_wa, acc_wb, acc_wt, acc_wd, acc_wx):
         acc[...] = jnp.zeros_like(acc)
 
+    not_mine = pl.ds((1 - core) * 16, 16)
+    mine = pl.ds(core * 16, 16)
+    own_s = x * Y + y
+    own_nb = pl.ds(own_s * nb, nb)
+    own_piece = pl.ds(core * 16 + own_s * nb, nb)
+    own_rows = pl.ds(pl.multiple_of(z * tile, tile), tile)
+
+    def reduce_core(copy, pieces, received, half, got):
+        copy.wait_recv()
+        half[...] = (pieces[mine].astype(F32) + received[...].astype(F32)).astype(BF)
+        return [
+            remote(half.at[pl.ds(s * nb, nb)], got.at[j], d) for j, (s, d) in enumerate(xy_peers)
+        ]
+
+    def sum_xy(copies, half, got):
+        for c in copies:
+            c.wait_recv()
+        total = half[own_nb].astype(F32)
+        for j in range(XY - 1):
+            total = total + got[j].astype(F32)
+        return total
+
+    def send_z(buffer, got):
+        return [
+            remote(buffer.at[:, pl.ds(pl.multiple_of(pz * tile, tile), tile)], got.at[j], d)
+            for j, (pz, d) in enumerate(z_peers)
+        ]
+
+    def sum_z(copies, buffer, got, whole):
+        for c in copies:
+            c.wait_recv()
+        total = buffer[:, own_rows]
+        for j in range(Z - 1):
+            total = total + got[j]
+        whole[:, own_rows] = total
+        return [remote(whole.at[:, own_rows], whole.at[:, own_rows], d) for _, d in z_peers]
+
+    def spread(full):
+        own = full.at[own_piece]
+        return [remote(own, own, d) for _, d in xy_peers], [remote(own, own, sib)]
+
+    def forward(copies, to_core, full):
+        for j, c in enumerate(copies):
+            c.wait_recv()
+            px = lax.rem(x + X - (j + 1) // Y, X)
+            py = lax.rem(y + Y - (j + 1) % Y, Y)
+            piece = full.at[pl.ds(core * 16 + (px * Y + py) * nb, nb)]
+            to_core.append(remote(piece, piece, sib))
+
+    def fold(acc, r, cols):
+        return (acc[16 * r : 16 * (r + 1), cols] + acc[DT + 16 * r : DT + 16 * (r + 1), cols]).astype(BF)
+
     def edge_mid(b, carry):
         at = block(b)
         mask = row_mask(b, WIDTH)
         cot = gather(dst_col[at], 0, cots).astype(BF)
-        atom_grad = nt(cot, wb[...])
-        summed = sm[at]
-        pre = inc[at] + nn(summed, wt2[...])
+        picked_cot[at] = cot
+        pre = inc[at] + nn(sm[at], wt2[...])
         sig = jax.nn.sigmoid(pre)
         out = jnp.where(mask, pre * sig, 0.0).astype(BF)
-        grad = jnp.where(mask, atom_grad * sig * (1.0 + pre * (1.0 - sig)), 0.0).astype(BF)
+        slope[at] = jnp.where(mask, sig * (1.0 + pre * (1.0 - sig)), 0.0)
+        acc_wb[...] += tn(out, cot)
+        return carry
+
+    lax.fori_loop(0, SLOTS // BLK, edge_mid, 0)
+    for s in range(32):
+        r, cols = s // 4, slice(128 * (s % 4), 128 * (s % 4 + 1))
+        pieces_b[s] = acc_wb[64 * r : 64 * (r + 1), cols].astype(BF)
+    b_core = remote(pieces_b.at[not_mine], rc_b, sib)
+
+    def edge_grad(b, carry):
+        at = block(b)
+        grad = (nt(picked_cot[at], wb[...]) * slope[at]).astype(BF)
         dpre[at] = grad
-        acc_wb[...] += tn(out, cot)
         acc_wa[...] += tn(picked[at], grad)
-        acc_wt[...] += tn(summed, grad)
+        acc_wt[...] += tn(sm[at], grad)
         down[at] = nt(grad, wt2[...]).astype(BF)
         return carry
 
-    lax.fori_loop(0, SLOTS // BLK, edge_mid, 0)
-
-    def fold(acc, r, cols):
-        return (acc[16 * r : 16 * (r + 1), cols] + acc[DT + 16 * r : DT + 16 * (r + 1), cols]).astype(BF)
+    lax.fori_loop(0, 2, edge_grad, 0)
+    b_xy = reduce_core(b_core, pieces_b, rc_b, half_b, rx_b)
+    lax.fori_loop(2, SLOTS // BLK, edge_grad, 0)
 
     for s in range(32):
-        r, c = (s % 16) // 4, s % 4
-        cols = slice(128 * c, 128 * (c + 1))
-        pieces[s, 0:128] = (acc_wa if s < 16 else acc_wb)[128 * r : 128 * (r + 1), cols].astype(BF)
-        pieces[s, 128:144] = fold(acc_wt, r, cols) if s < 16 else jnp.zeros((16, 128), BF)
-    not_mine = pl.ds((1 - core) * 16, 16)
-    mine = pl.ds(core * 16, 16)
-    w_core = remote(pieces.at[not_mine], rc, sib)
+        r, cols = s // 4, slice(128 * (s % 4), 128 * (s % 4 + 1))
+        pieces_a[s, 0:64] = acc_wa[64 * r : 64 * (r + 1), cols].astype(BF)
+        pieces_a[s, 64:80] = fold(acc_wt, r, cols) if s < 16 else jnp.zeros((16, 128), BF)
+    a_core = remote(pieces_a.at[not_mine], rc_a, sib)
 
     def table_grad(owner, source, out, who):
         for part in range(2):
@@ -323,21 +383,25 @@
 
     table_grad(1 - core, dpre, dt, 0)
     d_core = remote(dt.at[0], rd, sib)
-    w_core.wait_recv()
-    half[...] = (pieces[mine].astype(F32) + rc[...].astype(F32)).astype(BF)
-    w_xy = [
-        remote(half.at[pl.ds(s * nb, nb)], rx.at[j], d) for j, (s, d) in enumerate(xy_peers)
-    ]
+    a_xy = reduce_core(a_core, pieces_a, rc_a, half_a, rx_a)
+    z_b[...] = sum_xy(b_xy, half_b, rx_b)
+    b_z = send_z(z_b, rz_b)
     table_grad(core, dpre, dt, 1)
     d_core.wait_recv()
     ed[...] = (dt[1, 1 - zl].astype(F32) + rd[1 - zl].astype(F32)).astype(BF)
     rim_part = pl.ds(0, OWN)
     mid_part = pl.ds(OWN, OWN)
+    g_bz = sum_z(b_z, z_b, rz_b, fz_b)
     d_rim = remote(ed.at[rim_part], re.at[rim_part], zpart)
 
     pack(down)
     triplets(tout_col, tin_col, 2)
     unpack()
+
+    for c in g_bz:
+        c.wait_recv()
+    full_b[own_piece] = fz_b[...].astype(BF)
+    g_bxy, g_bcore = spread(full_b)
 
     def edge_out(b, carry):
         at = block(b)
@@ -351,53 +415,31 @@
     for s in range(32):
         r, c = (s % 16) // 4, s % 4
         late[s] = fold(acc_wd if s < 16 else acc_wx, r, slice(128 * c, 128 * (c + 1)))
-    l_core = remote(late.at[not_mine], rc2, sib)
+    l_core = remote(late.at[not_mine], rc_l, sib)
+
+    total_a = sum_xy(a_xy, half_a, rx_a)
+    z_a[...] = total_a[:, 0:64]
+    small_z[:, 0:16] = total_a[:, 64:80].astype(BF)
+    a_z = send_z(z_a, rz_a)
+    d_mid = remote(ed.at[mid_part], re.at[mid_part], zpart)
+
     table_grad(1 - core, sm, dt2, 0)
     d2_core = remote(dt2.at[0], rd2, sib)
-    l_core.wait_recv()
-    half2[...] = (late[mine].astype(F32) + rc2[...].astype(F32)).astype(BF)
-    l_xy = [
-        remote(half2.at[pl.ds(s * nb, nb)], rx2.at[j], d) for j, (s, d) in enumerate(xy_peers)
-    ]
-
-    own_s = x * Y + y
-    own_rows = pl.ds(pl.multiple_of(z * tile, tile), tile)
-    own_piece = pl.ds(core * 16 + own_s * nb, nb)
-
-    def sum_xy(copies, buffer, received):
-        for c in copies:
-            c.wait_recv()
-        total = buffer[pl.ds(own_s * nb, nb)].astype(F32)
-        for j in range(XY - 1):
-            total = total + received[j].astype(F32)
-        return total.astype(BF)
-
-    zbuf[:, 0:144] = sum_xy(w_xy, half, rx)
-    w_z = []
-    for j, (pz, d) in enumerate(z_peers):
-        part = pl.ds(pl.multiple_of(pz * tile, tile), tile)
-        w_z.append(remote(zbuf.at[:, part], rz_main.at[j + 1], d))
-    d_mid = remote(ed.at[mid_part], re.at[mid_part], zpart)
-
+    l_xy = reduce_core(l_core, late, rc_l, half_l, rx_l)
+    g_az = sum_z(a_z, z_a, rz_a, fz_a)
     table_grad(core, sm, dt2, 1)
-    zbuf[:, 144:160] = sum_xy(l_xy, half2, rx2)
-    l_z = [
-        remote(zbuf.at[:, pl.ds(128, 32)], rz_small.at[j + 1], d) for j, (_, d) in enumerate(z_peers)
-    ]
-    rz_small[0] = zbuf[:, 128:160]
+
+    small_z[:, 16:32] = sum_xy(l_xy, half_l, rx_l).astype(BF)
+    l_z = [remote(small_z, rz_small.at[j + 1], d) for j, (_, d) in enumerate(z_peers)]
+    rz_small[0] = small_z[...]
+
+    def narrow_pack(v):
+        v = v + pltpu.roll(v, DT, 1)
+        return jnp.where(lanes((OWN, 128)) < DT, v[0:OWN], v[OWN:])
+
     d2_core.wait_recv()
-    ed2[...] = (dt2[1, 1 - zl].astype(F32) + rd2[1 - zl].astype(F32)).astype(BF)
+    ed2[...] = narrow_pack(dt2[1, 1 - zl].astype(F32) + rd2[1 - zl].astype(F32)).astype(BF)
     d2_z = remote(ed2, re2, zpart)
-
-    for c in w_z:
-        c.wait_recv()
-    total = zbuf[:, own_rows].astype(F32)
-    for j in range(1, Z):
-        total = total + rz_main[j].astype(F32)
-    full[own_piece, own_rows] = total.astype(BF)
-    g_z = [
-        remote(full.at[own_piece, own_rows], full.at[own_piece, own_rows], d) for _, d in z_peers
-    ]
 
     d_rim.wait_recv()
     rims_out[...] = (
@@ -411,29 +453,30 @@
     small = rz_small[lax.rem(Z - z, Z)].astype(F32)
     for j in range(1, Z):
         small = small + rz_small[lax.rem(j + Z - z, Z)].astype(F32)
-    full[own_piece, 128:160] = small.astype(BF)
-    for c in g_z:
+    for c in g_az:
         c.wait_recv()
-    g_xy = [remote(full.at[own_piece], full.at[own_piece], d) for _, d in xy_peers]
-    g_core = [remote(full.at[own_piece], full.at[own_piece], sib)]
+    full_a[own_piece, 0:64] = fz_a[...].astype(BF)
+    full_a[own_piece, 64:96] = small.astype(BF)
+    g_axy, g_acore = spread(full_a)
+    forward(g_bxy, g_bcore, full_b)
 
     d2_z.wait_recv()
-    sum2 = dt2[1, zl].astype(F32) + rd2[zl].astype(F32) + re2[...].astype(F32)
-    rims2_out[...] = sum2[0:OWN].astype(BF)
+    sum2 = narrow_pack(dt2[1, zl].astype(F32) + rd2[zl].astype(F32)) + re2[...].astype(F32)
+    is_rim = lanes((OWN, 128)) < DT
+    rims2_out[...] = jnp.where(is_rim, sum2, 0.0).astype(BF)
     to_tails2 = remote(rims2_out.at[low], rims2_in.at[0], below)
     to_heads2 = remote(rims2_out.at[high], rims2_in.at[1], above)
-
-    for j, c in enumerate(g_xy):
+    for c in g_bcore:
         c.wait_recv()
-        px = lax.rem(x + X - (j + 1) // Y, X)
-        py = lax.rem(y + Y - (j + 1) % Y, Y)
-        piece = pl.ds(core * 16 + (px * Y + py) * nb, nb)
-        g_core.append(remote(full.at[piece], full.at[piece], sib))
+    b_copy = pltpu.make_async_copy(full_b, full_b_out, local_sem.at[8])
+    b_copy.start()
+    forward(g_axy, g_acore, full_a)
 
     d_mid.wait_recv()
     for c in (to_tails, to_heads, to_tails2, to_heads2):
         c.wait_recv()
-    narrow = sum2[OWN:] + jnp.concatenate([rims2_in[1].astype(F32), rims2_in[0].astype(F32)], axis=0)
+    rims2 = jnp.concatenate([rims2_in[1].astype(F32), rims2_in[0].astype(F32)], axis=0)
+    narrow = jnp.where(is_rim, 0.0, sum2) + rims2
     dproj = dt[1, zl, mid_part].astype(F32) + rd[zl, mid_part].astype(F32) + re[mid_part].astype(F32)
     dproj = dproj + jnp.concatenate([rims_in[1].astype(F32), rims_in[0].astype(F32)], axis=0)
     dproj = dproj + nn(narrow.astype(BF), wdown2[...])
@@ -443,19 +486,20 @@
     grad_copy = pltpu.make_async_copy(grad, grad_out, local_sem.at[6])
     grad_copy.start()
 
-    for c in g_core:
+    for c in g_acore:
         c.wait_recv()
-    full_copy = pltpu.make_async_copy(full, full_out, local_sem.at[7])
-    full_copy.start()
+    a_copy = pltpu.make_async_copy(full_a, full_a_out, local_sem.at[7])
+    a_copy.start()
     for c in started:
         c.wait_send()
+    b_copy.wait()
     grad_copy.wait()
-    full_copy.wait()
+    a_copy.wait()
 
 
 def finish(
-    factor, grad_hbm, full_hbm, wdown_ref, gatoms_hbm, gwa_hbm, gwd_hbm, gwt_hbm, gwb_hbm,
-    full, gwa, gwd, gwt, gwb, sem,
+    factor, grad_hbm, full_a_hbm, full_b_hbm, wdown_ref, gatoms_hbm, gwa_hbm, gwd_hbm, gwt_hbm, gwb_hbm,
+    full_a, full_b, grad, gwa, gwd, gwt, gwb, sem,
 ):
     copies = []
 
@@ -465,31 +509,36 @@
         copies.append(c)
         return c
 
-    second = copy(full_hbm.at[pl.ds(16, 16)], full.at[pl.ds(16, 16)])
-    first = copy(full_hbm.at[pl.ds(0, 16)], full.at[pl.ds(0, 16)])
-    copy(grad_hbm, gatoms_hbm)
-
-    def rows_of(first, part):
-        return jnp.concatenate(
-            [
-                jnp.concatenate([full[first + 4 * r + c, part] for c in range(4)], axis=1)
-                for r in range(4)
-            ],
-            axis=0,
-        )
-
-    second.wait()
-    gwb[...] = rows_of(16, slice(0, 128)).astype(F32) * factor
-    copy(gwb, gwb_hbm)
-    back = tn(rows_of(16, slice(144, 160)), wdown_ref[...])
-    first.wait()
-    gwa[...] = (rows_of(0, slice(0, 128)).astype(F32) + back) * factor
-    copy(gwa, gwa_hbm)
-    gwt[...] = rows_of(0, slice(128, 144)).astype(F32) * factor
+    loads_b = [copy(full_b_hbm.at[pl.ds(16 * i, 16)], full_b.at[pl.ds(16 * i, 16)]) for i in range(2)]
+    loads_a = [copy(full_a_hbm.at[pl.ds(16 * i, 16)], full_a.at[pl.ds(16 * i, 16)]) for i in range(2)]
+    through = copy(grad_hbm, grad)
+    loaded = len(copies)
+
+    def rows_of(full, s, part):
+        return jnp.concatenate([full[s + c, part].astype(F32) for c in range(4)], axis=1)
+
+    for i in range(2):
+        loads_b[i].wait()
+        for r in range(4 * i, 4 * i + 4):
+            gwb[64 * r : 64 * (r + 1)] = rows_of(full_b, 4 * r, slice(0, 64)) * factor
+        copy(gwb.at[pl.ds(256 * i, 256)], gwb_hbm.at[pl.ds(256 * i, 256)])
+    for c in loads_a:
+        c.wait()
+    back = jnp.concatenate([rows_of(full_a, 16 + 4 * r, slice(80, 96)) for r in range(4)], axis=0)
+    back = tn(back.astype(BF), wdown_ref[...])
+    for i in range(2):
+        for r in range(4 * i, 4 * i + 4):
+            main = rows_of(full_a, 4 * r, slice(0, 64))
+            gwa[64 * r : 64 * (r + 1)] = (main + back[64 * r : 64 * (r + 1)]) * factor
+        copy(gwa.at[pl.ds(256 * i, 256)], gwa_hbm.at[pl.ds(256 * i, 256)])
+    for r in range(4):
+        gwt[16 * r : 16 * (r + 1)] = rows_of(full_a, 4 * r, slice(64, 80)) * factor
+        gwd[16 * r : 16 * (r + 1)] = rows_of(full_a, 4 * r, slice(80, 96)) * factor
     copy(gwt, gwt_hbm)
-    gwd[...] = rows_of(0, slice(144, 160)).astype(F32) * factor
     copy(gwd, gwd_hbm)
-    for c in copies[2:]:
+    through.wait()
+    copy(grad, gatoms_hbm)
+    for c in copies[loaded:]:
         c.wait()
 
 
@@ -501,21 +550,22 @@
     dims = dims_of(slabs)
     Y, ZH, X = dims
     XY, Z = X * Y, 2 * ZH
-    nb, tile = 16 // XY, 128 // Z
-    transfers = 32 + 4 * (XY - 1) + 3 * (Z - 1)
+    nb, tile = 16 // XY, 64 // Z
+    transfers = 40 + 7 * (XY - 1) + 5 * (Z - 1)
     vmem = pl.BlockSpec(memory_space=pltpu.VMEM)
     hbm = pl.BlockSpec(memory_space=pl.ANY)
     index = [a.reshape(16, 128) for a in (edge_src, edge_dst, trip_in, trip_out)]
     w_down = w_down.T
     V = pltpu.VMEM
-    full, grad = pl.pallas_call(
+    full_a, full_b, grad = pl.pallas_call(
         functools.partial(kernel, dims),
         out_shape=(
-            jax.ShapeDtypeStruct((32, 160, 128), BF),
+            jax.ShapeDtypeStruct((32, 96, 128), BF),
+            jax.ShapeDtypeStruct((32, 64, 128), BF),
             jax.ShapeDtypeStruct((OWN, WIDTH), BF),
         ),
         in_specs=[vmem] * 8 + [hbm] * 6,
-        out_specs=(hbm, hbm),
+        out_specs=(hbm, hbm, hbm),
         scratch_shapes=[
             V((4, OWN, WIDTH), BF), V((4, OWN, WIDTH), BF), V((4, OWN, WIDTH), BF),
             V((SLOTS, WIDTH), BF), V((DT, SLOTS), BF), V((512, WIDTH), BF), V((512, WIDTH), BF),
@@ -526,16 +576,19 @@
             V((SLOTS, 128), BF), V((LO, WIDTH), BF), V((LO, WIDTH), F32), V((SLOTS, 128), BF),
             V((2, 2, ROWS, WIDTH), BF), V((2, ROWS, WIDTH), BF), V((ROWS, WIDTH), BF), V((ROWS, WIDTH), BF),
             V((OWN, WIDTH), BF),
-            V((2, 2, ROWS, 128), BF), V((2, ROWS, 128), BF), V((ROWS, 128), BF), V((ROWS, 128), BF),
+            V((2, 2, ROWS, 128), BF), V((2, ROWS, 128), BF), V((OWN, 128), BF), V((OWN, 128), BF),
             V((OWN, WIDTH), BF), V((2, GH, WIDTH), BF), V((OWN, 128), BF), V((2, GH, 128), BF),
             V((512, WIDTH), F32), V((512, WIDTH), F32), V((128, WIDTH), F32), V((128, WIDTH), F32),
             V((128, WIDTH), F32),
-            V((32, 144, 128), BF), V((16, 144, 128), BF), V((16, 144, 128), BF),
-            V((XY - 1, nb, 144, 128), BF),
+            V((SLOTS, WIDTH), BF), V((SLOTS, WIDTH), F32),
+            V((32, 64, 128), BF), V((16, 64, 128), BF), V((16, 64, 128), BF), V((XY - 1, nb, 64, 128), BF),
+            V((nb, 64, 128), F32), V((Z - 1, nb, tile, 128), F32), V((nb, 64, 128), F32), V((32, 64, 128), BF),
+            V((32, 80, 128), BF), V((16, 80, 128), BF), V((16, 80, 128), BF), V((XY - 1, nb, 80, 128), BF),
+            V((nb, 64, 128), F32), V((Z - 1, nb, tile, 128), F32), V((nb, 64, 128), F32), V((32, 96, 128), BF),
             V((32, 16, 128), BF), V((16, 16, 128), BF), V((16, 16, 128), BF), V((XY - 1, nb, 16, 128), BF),
-            V((nb, 160, 128), BF), V((Z, nb, tile, 128), BF), V((Z, nb, 32, 128), BF), V((32, 160, 128), BF),
+            V((nb, 32, 128), BF), V((Z, nb, 32, 128), BF),
             pltpu.SemaphoreType.DMA((transfers,)), pltpu.SemaphoreType.DMA((transfers,)),
-            pltpu.SemaphoreType.DMA((8,)),
+            pltpu.SemaphoreType.DMA((9,)),
         ],
         compiler_params=pltpu.CompilerParams(
             collective_id=0, has_side_effects=True, vmem_limit_bytes=60 * 1024 * 1024
@@ -554,14 +607,14 @@
             jax.ShapeDtypeStruct((DT, WIDTH), F32),
             jax.ShapeDtypeStruct((512, WIDTH), F32),
         ),
-        in_specs=[hbm, hbm, vmem],
+        in_specs=[hbm, hbm, hbm, vmem],
         out_specs=(hbm,) * 5,
         scratch_shapes=[
-            V((32, 160, 128), BF), V((512, WIDTH), F32), V((DT, WIDTH), F32), V((DT, WIDTH), F32),
-            V((512, WIDTH), F32), pltpu.SemaphoreType.DMA((8,)),
+            V((32, 96, 128), BF), V((32, 64, 128), BF), V((OWN, WIDTH), BF), V((512, WIDTH), F32),
+            V((DT, WIDTH), F32), V((DT, WIDTH), F32), V((512, WIDTH), F32), pltpu.SemaphoreType.DMA((12,)),
         ],
         compiler_params=pltpu.CompilerParams(vmem_limit_bytes=60 * 1024 * 1024),
-    )(grad, full, w_down)
+    )(grad, full_a, full_b, w_down)
     return grad, gwa, gwd.T, gwt, gwb
 
 

time: 107 us -> 99.4 us (0.929)
  Pallas kernels: 105 us -> 97.1 us
    pallas_call x1, Pallas kernels: 9.96 us -> 3.61 us  [per_device(): pl.pallas_call(functools.partial(finish, factor), out_shape=(jax.ShapeDty...]
    pallas_call x1, Pallas kernels: 94.7 us -> 93.5 us  [per_device(): pl.pallas_call(functools.partial(kernel, dims), out_shape=(jax.ShapeDtype...]
where the time goes in v4:
time: 99.4 us; the launch traced here: 99.2 us
  Pallas kernels  97.1 us (98%)
  between operations  2.1 us (2%)
    pallas_call x1, Pallas kernels, per_device(): pl.pallas_call(functools.partial(kernel, dims), out_shape=(jax.ShapeDtype...  93.5 us
    pallas_call x1, Pallas kernels, per_device(): pl.pallas_call(functools.partial(finish, factor), out_shape=(jax.ShapeDty...  3.61 us

profile of v4, /device:TPU:1, one launch (start us, length us, event | category | flops | bytes accessed | tf_op | source)
XLA Modules:
  0.0 99.2 jit_solution(9235234598353741778)
XLA Ops:
  1.9 93.5 %shard_map.173 = (bf16[32,96,128]{2,1,0:T(8,128)(2,1)}, bf16[32,64,128]{2,1,0:T(8,128)(2,1)}, bf16[256,512]{1,0:T(8,128)(2,1)}) custom-call(s32[1,1]{1,0:T(1,128)} %bitcast.9.ecnt_ref, s32[1,1]{1,0:T(1,128)} %bitcast.10.tcnt_ref, s32[16,128]{1,0:T(8,128)} %bitcast.14, s32[16,128]{1,0:T(8,128)} %bitcast.15, s32[16,128]{1,0:T(8,128)} %bitcast.16, ...), custom_call_target="tpu_custom_call" | custom-call | tf_op jit(solution)/shard_map/pallas_call | solution.py:560
  95.4 3.6 %shard_map.174 = (bf16[256,512]{1,0:T(8,128)(2,1)}, f32[512,512]{1,0:T(8,128)}, f32[64,512]{1,0:T(8,128)}, f32[64,512]{1,0:T(8,128)}, f32[512,512]{1,0:T(8,128)}) custom-call(bf16[256,512]{1,0:T(8,128)(2,1)} %get-tuple-element.13.grad_hbm, bf16[32,96,128]{2,1,0:T(8,128)(2,1)} %get-tuple-element.14.full_a_hbm, ...), custom_call_target="tpu_custom_call" | custom-call | tf_op jit(solution)/shard_map/pallas_call | solution.py:601

commit v5 on v4

--- a/solution.py
+++ b/solution.py
@@ -13,7 +13,6 @@
 MESH = pl.DeviceIdType.MESH
 GH = 128
 OWN = 256
-ROWS = 512
 SLOTS = 2048
 WIDTH = 512
 DT = 64
@@ -67,21 +66,20 @@
     ecnt_ref, tcnt_ref, src_ref, dst_ref, tin_ref, tout_ref, wdown_ref, wt_ref,
     atoms_hbm, cot_hbm, msg_hbm, basis_hbm, wa_hbm, wb_hbm,
     full_a_out, full_b_out, grad_out,
-    mid, rim, cots, msg, basis, wa, wb, picked, inc, dpre,
+    mid, rim, cots, msg, basis, wa, wb, picked, inc, dinc,
     src_col, dst_col, tin_col, tout_col, rows, basis2, wdown2, wt2,
     down, dn, acc_s, sm,
-    dt, rd, ed, re, grad, dt2, rd2, ed2, re2, rims_out, rims_in, rims2_out, rims2_in,
+    dt_sib, dt, rd, ed, re, grad, rims_out, rims_in,
     acc_wa, acc_wb, acc_wt, acc_wd, acc_wx, picked_cot, slope,
-    pieces_b, rc_b, half_b, rx_b, z_b, rz_b, fz_b, full_b,
-    pieces_a, rc_a, half_a, rx_a, z_a, rz_a, fz_a, full_a,
-    late, rc_l, half_l, rx_l, small_z, rz_small,
+    pieces_b, rc_b, half_b, rx_b, rz_b, full_b,
+    pieces_a, rc_a, half_a, rx_a, rz_a, full_a,
+    late, rc_l, half_l, rx_l, rz_l,
     send, recv, local_sem,
 ):
     Y, ZH, X = dims
     XY = X * Y
     Z = 2 * ZH
     nb = 16 // XY
-    tile = 64 // Z
     dom = lax.axis_index("dom")
     gp = lax.axis_index("gp")
     slabs = Y * ZH * X
@@ -105,10 +103,10 @@
     z_peers = []
     for j in range(1, Z):
         pz = lax.rem(z + j, Z)
-        z_peers.append((pz, {"dom": (y * ZH + lax.div(pz, 2)) * X + x, "gp": lax.rem(pz, 2) * 2 + core}))
+        z_peers.append({"dom": (y * ZH + lax.div(pz, 2)) * X + x, "gp": lax.rem(pz, 2) * 2 + core})
 
     barrier = pltpu.get_barrier_semaphore()
-    others = [sib, above, below] + [d for _, d in xy_peers] + [d for _, d in z_peers]
+    others = [sib, above, below] + [d for _, d in xy_peers] + z_peers
     for d in others:
         pl.semaphore_signal(barrier, inc=1, device_id=d, device_id_type=MESH)
 
@@ -238,7 +236,7 @@
             sm[2 * j * LO : (2 * j + 1) * LO] = jnp.where(first, v, 0.0).astype(BF)
             sm[(2 * j + 1) * LO : (2 * j + 2) * LO] = jnp.where(first, 0.0, v).astype(BF)
 
-    def triplets(from_col, to_col, to_row):
+    def triplets(from_col, to_col, to_row, between=lambda: None):
         half_lane = jnp.where(lanes((BLK, 128)) < DT, 0, 1)
         acc_s[...] = jnp.zeros_like(acc_s)
 
@@ -263,7 +261,10 @@
             acc_s[...] += nn(pick_rows(line & (LO - 1), 0, LO), spread)
             return carry
 
-        lax.fori_loop(0, SLOTS // BLK, body, 0)
+        lax.fori_loop(0, 2, body, 0)
+        result = between()
+        lax.fori_loop(2, SLOTS // BLK, body, 0)
+        return result
 
     pack(down)
     triplets(tin_col, tout_col, 3)
@@ -281,7 +282,6 @@
     own_s = x * Y + y
     own_nb = pl.ds(own_s * nb, nb)
     own_piece = pl.ds(core * 16 + own_s * nb, nb)
-    own_rows = pl.ds(pl.multiple_of(z * tile, tile), tile)
 
     def reduce_core(copy, pieces, received, half, got):
         copy.wait_recv()
@@ -298,20 +298,17 @@
             total = total + got[j].astype(F32)
         return total
 
-    def send_z(buffer, got):
-        return [
-            remote(buffer.at[:, pl.ds(pl.multiple_of(pz * tile, tile), tile)], got.at[j], d)
-            for j, (pz, d) in enumerate(z_peers)
-        ]
-
-    def sum_z(copies, buffer, got, whole):
+    def send_z(own, got):
+        got[0] = own.astype(BF)
+        return [remote(got.at[0], got.at[j + 1], d) for j, d in enumerate(z_peers)]
+
+    def sum_z(copies, got):
         for c in copies:
             c.wait_recv()
-        total = buffer[:, own_rows]
-        for j in range(Z - 1):
-            total = total + got[j]
-        whole[:, own_rows] = total
-        return [remote(whole.at[:, own_rows], whole.at[:, own_rows], d) for _, d in z_peers]
+        total = got[lax.rem(Z - z, Z)].astype(F32)
+        for j in range(1, Z):
+            total = total + got[lax.rem(j + Z - z, Z)].astype(F32)
+        return total.astype(BF)
 
     def spread(full):
         own = full.at[own_piece]
@@ -348,8 +345,9 @@
 
     def edge_grad(b, carry):
         at = block(b)
-        grad = (nt(picked_cot[at], wb[...]) * slope[at]).astype(BF)
-        dpre[at] = grad
+        grad = nt(picked_cot[at], wb[...]) * slope[at]
+        slope[at] = grad
+        grad = grad.astype(BF)
         acc_wa[...] += tn(picked[at], grad)
         acc_wt[...] += tn(sm[at], grad)
         down[at] = nt(grad, wt2[...]).astype(BF)
@@ -365,48 +363,17 @@
         pieces_a[s, 64:80] = fold(acc_wt, r, cols) if s < 16 else jnp.zeros((16, 128), BF)
     a_core = remote(pieces_a.at[not_mine], rc_a, sib)
 
-    def table_grad(owner, source, out, who):
-        for part in range(2):
-            first = (4 + owner) * OWN if part == 0 else owner * OWN
-            total = None
-            for b in range(SLOTS // BLK):
-                cols = slice(BLK * b, BLK * (b + 1))
-                line = rows[0:1, cols]
-                choice = jnp.concatenate(
-                    [pick_rows(line, first, OWN), pick_rows(line, first + 2 * OWN, OWN)], axis=0
-                )
-                term = nn(choice, source[cols])
-                total = term if total is None else total + term
-            total = total.astype(BF)
-            out[who, 0, OWN * part : OWN * (part + 1)] = total[0:OWN]
-            out[who, 1, OWN * part : OWN * (part + 1)] = total[OWN:]
-
-    table_grad(1 - core, dpre, dt, 0)
-    d_core = remote(dt.at[0], rd, sib)
-    a_xy = reduce_core(a_core, pieces_a, rc_a, half_a, rx_a)
-    z_b[...] = sum_xy(b_xy, half_b, rx_b)
-    b_z = send_z(z_b, rz_b)
-    table_grad(core, dpre, dt, 1)
-    d_core.wait_recv()
-    ed[...] = (dt[1, 1 - zl].astype(F32) + rd[1 - zl].astype(F32)).astype(BF)
-    rim_part = pl.ds(0, OWN)
-    mid_part = pl.ds(OWN, OWN)
-    g_bz = sum_z(b_z, z_b, rz_b, fz_b)
-    d_rim = remote(ed.at[rim_part], re.at[rim_part], zpart)
-
     pack(down)
-    triplets(tout_col, tin_col, 2)
+    a_xy = triplets(
+        tout_col, tin_col, 2, lambda: reduce_core(a_core, pieces_a, rc_a, half_a, rx_a)
+    )
     unpack()
-
-    for c in g_bz:
-        c.wait_recv()
-    full_b[own_piece] = fz_b[...].astype(BF)
-    g_bxy, g_bcore = spread(full_b)
 
     def edge_out(b, carry):
         at = block(b)
-        back = jnp.where(row_mask(b, 128), sm[at].astype(F32), 0.0).astype(BF)
-        sm[at] = back
+        mask = row_mask(b, 128)
+        back = jnp.where(mask, sm[at].astype(F32), 0.0).astype(BF)
+        dinc[at] = (slope[at] + nn(back, wdown2[...])).astype(BF)
         acc_wd[...] += tn(back, inc[at].astype(BF))
         acc_wx[...] += tn(back, picked[at])
         return carry
@@ -417,69 +384,64 @@
         late[s] = fold(acc_wd if s < 16 else acc_wx, r, slice(128 * c, 128 * (c + 1)))
     l_core = remote(late.at[not_mine], rc_l, sib)
 
-    total_a = sum_xy(a_xy, half_a, rx_a)
-    z_a[...] = total_a[:, 0:64]
-    small_z[:, 0:16] = total_a[:, 64:80].astype(BF)
-    a_z = send_z(z_a, rz_a)
-    d_mid = remote(ed.at[mid_part], re.at[mid_part], zpart)
-
-    table_grad(1 - core, sm, dt2, 0)
-    d2_core = remote(dt2.at[0], rd2, sib)
+    def table_grad(owner, part, out):
+        first = (4 + owner) * OWN if part == 0 else owner * OWN
+        total = None
+        for b in range(SLOTS // BLK):
+            cols = slice(BLK * b, BLK * (b + 1))
+            line = rows[0:1, cols]
+            choice = jnp.concatenate(
+                [pick_rows(line, first, OWN), pick_rows(line, first + 2 * OWN, OWN)], axis=0
+            )
+            term = nn(choice, dinc[cols])
+            total = term if total is None else total + term
+        total = total.astype(BF)
+        out[part, 0] = total[0:OWN]
+        out[part, 1] = total[OWN:]
+
+    def reduce_slot(part):
+        ed[part] = (dt[part, 1 - zl].astype(F32) + rd[part, 1 - zl].astype(F32)).astype(BF)
+        return remote(ed.at[part], re.at[part], zpart)
+
+    def slot_sum(part):
+        return dt[part, zl].astype(F32) + rd[part, zl].astype(F32) + re[part].astype(F32)
+
+    table_grad(1 - core, 0, dt_sib)
+    rim_core = remote(dt_sib.at[0], rd.at[0], sib)
+    rz = send_z(sum_xy(b_xy, half_b, rx_b), rz_b)
+    table_grad(core, 0, dt)
     l_xy = reduce_core(l_core, late, rc_l, half_l, rx_l)
-    g_az = sum_z(a_z, z_a, rz_a, fz_a)
-    table_grad(core, sm, dt2, 1)
-
-    small_z[:, 16:32] = sum_xy(l_xy, half_l, rx_l).astype(BF)
-    l_z = [remote(small_z, rz_small.at[j + 1], d) for j, (_, d) in enumerate(z_peers)]
-    rz_small[0] = small_z[...]
-
-    def narrow_pack(v):
-        v = v + pltpu.roll(v, DT, 1)
-        return jnp.where(lanes((OWN, 128)) < DT, v[0:OWN], v[OWN:])
-
-    d2_core.wait_recv()
-    ed2[...] = narrow_pack(dt2[1, 1 - zl].astype(F32) + rd2[1 - zl].astype(F32)).astype(BF)
-    d2_z = remote(ed2, re2, zpart)
-
-    d_rim.wait_recv()
-    rims_out[...] = (
-        dt[1, zl, rim_part].astype(F32) + rd[zl, rim_part].astype(F32) + re[rim_part].astype(F32)
-    ).astype(BF)
+    rim_core.wait_recv()
+    rim_z = reduce_slot(0)
+    table_grad(1 - core, 1, dt_sib)
+    mid_core = remote(dt_sib.at[1], rd.at[1], sib)
+    a_z = send_z(sum_xy(a_xy, half_a, rx_a), rz_a)
+    table_grad(core, 1, dt)
+    full_b[own_piece] = sum_z(rz, rz_b)
+    g_bxy, g_bcore = spread(full_b)
+    l_z = send_z(sum_xy(l_xy, half_l, rx_l), rz_l)
+    mid_core.wait_recv()
+    mid_z = reduce_slot(1)
+
+    rim_z.wait_recv()
+    rims_out[...] = slot_sum(0).astype(BF)
     to_tails = remote(rims_out.at[low], rims_in.at[0], below)
     to_heads = remote(rims_out.at[high], rims_in.at[1], above)
 
-    for c in l_z:
-        c.wait_recv()
-    small = rz_small[lax.rem(Z - z, Z)].astype(F32)
-    for j in range(1, Z):
-        small = small + rz_small[lax.rem(j + Z - z, Z)].astype(F32)
-    for c in g_az:
-        c.wait_recv()
-    full_a[own_piece, 0:64] = fz_a[...].astype(BF)
-    full_a[own_piece, 64:96] = small.astype(BF)
+    full_a[own_piece, 0:80] = sum_z(a_z, rz_a)
+    full_a[own_piece, 80:96] = sum_z(l_z, rz_l)
     g_axy, g_acore = spread(full_a)
     forward(g_bxy, g_bcore, full_b)
-
-    d2_z.wait_recv()
-    sum2 = narrow_pack(dt2[1, zl].astype(F32) + rd2[zl].astype(F32)) + re2[...].astype(F32)
-    is_rim = lanes((OWN, 128)) < DT
-    rims2_out[...] = jnp.where(is_rim, sum2, 0.0).astype(BF)
-    to_tails2 = remote(rims2_out.at[low], rims2_in.at[0], below)
-    to_heads2 = remote(rims2_out.at[high], rims2_in.at[1], above)
     for c in g_bcore:
         c.wait_recv()
     b_copy = pltpu.make_async_copy(full_b, full_b_out, local_sem.at[8])
     b_copy.start()
     forward(g_axy, g_acore, full_a)
 
-    d_mid.wait_recv()
-    for c in (to_tails, to_heads, to_tails2, to_heads2):
-        c.wait_recv()
-    rims2 = jnp.concatenate([rims2_in[1].astype(F32), rims2_in[0].astype(F32)], axis=0)
-    narrow = jnp.where(is_rim, 0.0, sum2) + rims2
-    dproj = dt[1, zl, mid_part].astype(F32) + rd[zl, mid_part].astype(F32) + re[mid_part].astype(F32)
-    dproj = dproj + jnp.concatenate([rims_in[1].astype(F32), rims_in[0].astype(F32)], axis=0)
-    dproj = dproj + nn(narrow.astype(BF), wdown2[...])
+    mid_z.wait_recv()
+    to_tails.wait_recv()
+    to_heads.wait_recv()
+    dproj = slot_sum(1) + jnp.concatenate([rims_in[1].astype(F32), rims_in[0].astype(F32)], axis=0)
     coarse = dproj.astype(BF)
     fine = (dproj - coarse.astype(F32)).astype(BF)
     grad[...] = (nt(coarse, wa[...]) + nt(fine, wa[...])).astype(BF)
@@ -550,7 +512,7 @@
     dims = dims_of(slabs)
     Y, ZH, X = dims
     XY, Z = X * Y, 2 * ZH
-    nb, tile = 16 // XY, 64 // Z
+    nb = 16 // XY
     transfers = 40 + 7 * (XY - 1) + 5 * (Z - 1)
     vmem = pl.BlockSpec(memory_space=pltpu.VMEM)
     hbm = pl.BlockSpec(memory_space=pl.ANY)
@@ -574,19 +536,18 @@
             V((SLOTS, 128), jnp.int32), V((SLOTS, 128), jnp.int32),
             V((8, SLOTS), jnp.int32), V((SLOTS, 128), F32), V((128, WIDTH), BF), V((128, WIDTH), BF),
             V((SLOTS, 128), BF), V((LO, WIDTH), BF), V((LO, WIDTH), F32), V((SLOTS, 128), BF),
-            V((2, 2, ROWS, WIDTH), BF), V((2, ROWS, WIDTH), BF), V((ROWS, WIDTH), BF), V((ROWS, WIDTH), BF),
-            V((OWN, WIDTH), BF),
-            V((2, 2, ROWS, 128), BF), V((2, ROWS, 128), BF), V((OWN, 128), BF), V((OWN, 128), BF),
-            V((OWN, WIDTH), BF), V((2, GH, WIDTH), BF), V((OWN, 128), BF), V((2, GH, 128), BF),
+            V((2, 2, OWN, WIDTH), BF), V((2, 2, OWN, WIDTH), BF), V((2, 2, OWN, WIDTH), BF),
+            V((2, OWN, WIDTH), BF), V((2, OWN, WIDTH), BF), V((OWN, WIDTH), BF),
+            V((OWN, WIDTH), BF), V((2, GH, WIDTH), BF),
             V((512, WIDTH), F32), V((512, WIDTH), F32), V((128, WIDTH), F32), V((128, WIDTH), F32),
             V((128, WIDTH), F32),
             V((SLOTS, WIDTH), BF), V((SLOTS, WIDTH), F32),
             V((32, 64, 128), BF), V((16, 64, 128), BF), V((16, 64, 128), BF), V((XY - 1, nb, 64, 128), BF),
-            V((nb, 64, 128), F32), V((Z - 1, nb, tile, 128), F32), V((nb, 64, 128), F32), V((32, 64, 128), BF),
+            V((Z, nb, 64, 128), BF), V((32, 64, 128), BF),
             V((32, 80, 128), BF), V((16, 80, 128), BF), V((16, 80, 128), BF), V((XY - 1, nb, 80, 128), BF),
-            V((nb, 64, 128), F32), V((Z - 1, nb, tile, 128), F32), V((nb, 64, 128), F32), V((32, 96, 128), BF),
+            V((Z, nb, 80, 128), BF), V((32, 96, 128), BF),
             V((32, 16, 128), BF), V((16, 16, 128), BF), V((16, 16, 128), BF), V((XY - 1, nb, 16, 128), BF),
-            V((nb, 32, 128), BF), V((Z, nb, 32, 128), BF),
+            V((Z, nb, 16, 128), BF),
             pltpu.SemaphoreType.DMA((transfers,)), pltpu.SemaphoreType.DMA((transfers,)),
             pltpu.SemaphoreType.DMA((9,)),
         ],

time: 99.4 us -> 94 us (0.946)
  Pallas kernels: 97.1 us -> 91.6 us
    pallas_call x1, Pallas kernels: 93.5 us -> 88 us  [per_device(): pl.pallas_call(functools.partial(kernel, dims), out_shape=(jax.ShapeDtype...]
where the time goes in v5:
time: 94 us; the launch traced here: 93.7 us
  Pallas kernels  91.6 us (97%)
  between operations  2.1 us (2%)
    pallas_call x1, Pallas kernels, per_device(): pl.pallas_call(functools.partial(kernel, dims), out_shape=(jax.ShapeDtype...  88 us
    pallas_call x1, Pallas kernels, per_device(): pl.pallas_call(functools.partial(finish, factor), out_shape=(jax.ShapeDty...  3.6 us

profile of v5, /device:TPU:1, one launch (start us, length us, event | category | flops | bytes accessed | tf_op | source)
XLA Modules:
  0.0 93.7 jit_solution(9226875571217598959)
XLA Ops:
  1.9 88.0 %shard_map.173 = (bf16[32,96,128]{2,1,0:T(8,128)(2,1)}, bf16[32,64,128]{2,1,0:T(8,128)(2,1)}, bf16[256,512]{1,0:T(8,128)(2,1)}) custom-call(s32[1,1]{1,0:T(1,128)} %bitcast.9.ecnt_ref, s32[1,1]{1,0:T(1,128)} %bitcast.10.tcnt_ref, s32[16,128]{1,0:T(8,128)} %bitcast.14, s32[16,128]{1,0:T(8,128)} %bitcast.15, s32[16,128]{1,0:T(8,128)} %bitcast.16, ...), custom_call_target="tpu_custom_call" | custom-call | tf_op jit(solution)/shard_map/pallas_call | solution.py:522
  90.0 3.6 %shard_map.174 = (bf16[256,512]{1,0:T(8,128)(2,1)}, f32[512,512]{1,0:T(8,128)}, f32[64,512]{1,0:T(8,128)}, f32[64,512]{1,0:T(8,128)}, f32[512,512]{1,0:T(8,128)}) custom-call(bf16[256,512]{1,0:T(8,128)(2,1)} %get-tuple-element.13.grad_hbm, bf16[32,96,128]{2,1,0:T(8,128)(2,1)} %get-tuple-element.14.full_a_hbm, ...), custom_call_target="tpu_custom_call" | custom-call | tf_op jit(solution)/shard_map/pallas_call | solution.py:562

commit v6 on v5

--- a/solution.py
+++ b/solution.py
@@ -70,6 +70,7 @@
     src_col, dst_col, tin_col, tout_col, rows, basis2, wdown2, wt2,
     down, dn, acc_s, sm,
     dt_sib, dt, rd, ed, re, grad, rims_out, rims_in,
+    nt_sib, ntd, nrd, ned, nre, rims2_out, rims2_in,
     acc_wa, acc_wb, acc_wt, acc_wd, acc_wx, picked_cot, slope,
     pieces_b, rc_b, half_b, rx_b, rz_b, full_b,
     pieces_a, rc_a, half_a, rx_a, rz_a, full_a,
@@ -174,7 +175,6 @@
     to_below.wait_recv()
     z_high = remote(rim.at[gp, high], rim.at[gp, high], zpart)
     s_high = remote(rim.at[gp, high], rim.at[gp, high], sib)
-    z_cot = remote(cot_hbm, cots.at[gp], zpart)
     s_cot = remote(cot_hbm, cots.at[gp], sib)
     to_z.wait_recv()
     f_mid = remote(mid.at[kz], mid.at[kz], sib)
@@ -199,6 +199,7 @@
     f_low = remote(rim.at[kz, low], rim.at[kz, low], sib)
     z_high.wait_recv()
     f_high = remote(rim.at[kz, high], rim.at[kz, high], sib)
+    z_cot = remote(cot_hbm, cots.at[gp], zpart)
     for c in (s_low, s_high, f_low, f_high):
         c.wait_recv()
     wa_in.wait()
@@ -219,8 +220,6 @@
         return carry
 
     lax.fori_loop(0, SLOTS // BLK, edge_in, 0)
-    z_cot.wait_recv()
-    f_cot = remote(cots.at[kz], cots.at[kz], sib)
 
     def pack(source):
         first = lanes((LO, 128)) < DT
@@ -236,7 +235,7 @@
             sm[2 * j * LO : (2 * j + 1) * LO] = jnp.where(first, v, 0.0).astype(BF)
             sm[(2 * j + 1) * LO : (2 * j + 2) * LO] = jnp.where(first, 0.0, v).astype(BF)
 
-    def triplets(from_col, to_col, to_row, between=lambda: None):
+    def triplets(from_col, to_col, to_row):
         half_lane = jnp.where(lanes((BLK, 128)) < DT, 0, 1)
         acc_s[...] = jnp.zeros_like(acc_s)
 
@@ -261,14 +260,13 @@
             acc_s[...] += nn(pick_rows(line & (LO - 1), 0, LO), spread)
             return carry
 
-        lax.fori_loop(0, 2, body, 0)
-        result = between()
-        lax.fori_loop(2, SLOTS // BLK, body, 0)
-        return result
+        lax.fori_loop(0, SLOTS // BLK, body, 0)
 
     pack(down)
     triplets(tin_col, tout_col, 3)
     unpack()
+    z_cot.wait_recv()
+    f_cot = remote(cots.at[kz], cots.at[kz], sib)
     cot_in.wait()
     wb_in.wait()
     s_cot.wait_recv()
@@ -310,16 +308,16 @@
             total = total + got[lax.rem(j + Z - z, Z)].astype(F32)
         return total.astype(BF)
 
-    def spread(full):
-        own = full.at[own_piece]
+    def spread(full, part):
+        own = full.at[own_piece, part]
         return [remote(own, own, d) for _, d in xy_peers], [remote(own, own, sib)]
 
-    def forward(copies, to_core, full):
+    def forward(copies, to_core, full, part):
         for j, c in enumerate(copies):
             c.wait_recv()
             px = lax.rem(x + X - (j + 1) // Y, X)
             py = lax.rem(y + Y - (j + 1) % Y, Y)
-            piece = full.at[pl.ds(core * 16 + (px * Y + py) * nb, nb)]
+            piece = full.at[pl.ds(core * 16 + (px * Y + py) * nb, nb), part]
             to_core.append(remote(piece, piece, sib))
 
     def fold(acc, r, cols):
@@ -348,6 +346,7 @@
         grad = nt(picked_cot[at], wb[...]) * slope[at]
         slope[at] = grad
         grad = grad.astype(BF)
+        dinc[at] = grad
         acc_wa[...] += tn(picked[at], grad)
         acc_wt[...] += tn(sm[at], grad)
         down[at] = nt(grad, wt2[...]).astype(BF)
@@ -363,28 +362,7 @@
         pieces_a[s, 64:80] = fold(acc_wt, r, cols) if s < 16 else jnp.zeros((16, 128), BF)
     a_core = remote(pieces_a.at[not_mine], rc_a, sib)
 
-    pack(down)
-    a_xy = triplets(
-        tout_col, tin_col, 2, lambda: reduce_core(a_core, pieces_a, rc_a, half_a, rx_a)
-    )
-    unpack()
-
-    def edge_out(b, carry):
-        at = block(b)
-        mask = row_mask(b, 128)
-        back = jnp.where(mask, sm[at].astype(F32), 0.0).astype(BF)
-        dinc[at] = (slope[at] + nn(back, wdown2[...])).astype(BF)
-        acc_wd[...] += tn(back, inc[at].astype(BF))
-        acc_wx[...] += tn(back, picked[at])
-        return carry
-
-    lax.fori_loop(0, SLOTS // BLK, edge_out, 0)
-    for s in range(32):
-        r, c = (s % 16) // 4, s % 4
-        late[s] = fold(acc_wd if s < 16 else acc_wx, r, slice(128 * c, 128 * (c + 1)))
-    l_core = remote(late.at[not_mine], rc_l, sib)
-
-    def table_grad(owner, part, out):
+    def table_grad(owner, part, source):
         first = (4 + owner) * OWN if part == 0 else owner * OWN
         total = None
         for b in range(SLOTS // BLK):
@@ -393,11 +371,9 @@
             choice = jnp.concatenate(
                 [pick_rows(line, first, OWN), pick_rows(line, first + 2 * OWN, OWN)], axis=0
             )
-            term = nn(choice, dinc[cols])
+            term = nn(choice, source[cols])
             total = term if total is None else total + term
-        total = total.astype(BF)
-        out[part, 0] = total[0:OWN]
-        out[part, 1] = total[OWN:]
+        return total.astype(BF).reshape(2, OWN, total.shape[1])
 
     def reduce_slot(part):
         ed[part] = (dt[part, 1 - zl].astype(F32) + rd[part, 1 - zl].astype(F32)).astype(BF)
@@ -406,49 +382,90 @@
     def slot_sum(part):
         return dt[part, zl].astype(F32) + rd[part, zl].astype(F32) + re[part].astype(F32)
 
-    table_grad(1 - core, 0, dt_sib)
+    dt_sib[0] = table_grad(1 - core, 0, dinc)
     rim_core = remote(dt_sib.at[0], rd.at[0], sib)
-    rz = send_z(sum_xy(b_xy, half_b, rx_b), rz_b)
-    table_grad(core, 0, dt)
-    l_xy = reduce_core(l_core, late, rc_l, half_l, rx_l)
+    a_xy = reduce_core(a_core, pieces_a, rc_a, half_a, rx_a)
+    dt[0] = table_grad(core, 0, dinc)
     rim_core.wait_recv()
     rim_z = reduce_slot(0)
-    table_grad(1 - core, 1, dt_sib)
+
+    pack(down)
+    triplets(tout_col, tin_col, 2)
+    unpack()
+
+    def edge_back(b, carry):
+        at = block(b)
+        back = jnp.where(row_mask(b, 128), sm[at].astype(F32), 0.0).astype(BF)
+        sm[at] = back
+        acc_wd[...] += tn(back, inc[at].astype(BF))
+        acc_wx[...] += tn(back, picked[at])
+        return carry
+
+    lax.fori_loop(0, SLOTS // BLK, edge_back, 0)
+    for s in range(32):
+        r, c = (s % 16) // 4, s % 4
+        late[s] = fold(acc_wd if s < 16 else acc_wx, r, slice(128 * c, 128 * (c + 1)))
+    l_core = remote(late.at[not_mine], rc_l, sib)
+
+    b_z = send_z(sum_xy(b_xy, half_b, rx_b), rz_b)
+
+    def edge_out(b, carry):
+        at = block(b)
+        dinc[at] = (slope[at] + nn(sm[at], wdown2[...])).astype(BF)
+        return carry
+
+    lax.fori_loop(0, SLOTS // BLK, edge_out, 0)
+    l_xy = reduce_core(l_core, late, rc_l, half_l, rx_l)
+    dt_sib[1] = table_grad(1 - core, 1, dinc)
     mid_core = remote(dt_sib.at[1], rd.at[1], sib)
-    a_z = send_z(sum_xy(a_xy, half_a, rx_a), rz_a)
-    table_grad(core, 1, dt)
-    full_b[own_piece] = sum_z(rz, rz_b)
-    g_bxy, g_bcore = spread(full_b)
-    l_z = send_z(sum_xy(l_xy, half_l, rx_l), rz_l)
-    mid_core.wait_recv()
-    mid_z = reduce_slot(1)
-
     rim_z.wait_recv()
     rims_out[...] = slot_sum(0).astype(BF)
     to_tails = remote(rims_out.at[low], rims_in.at[0], below)
     to_heads = remote(rims_out.at[high], rims_in.at[1], above)
-
-    full_a[own_piece, 0:80] = sum_z(a_z, rz_a)
-    full_a[own_piece, 80:96] = sum_z(l_z, rz_l)
-    g_axy, g_acore = spread(full_a)
-    forward(g_bxy, g_bcore, full_b)
+    a_z = send_z(sum_xy(a_xy, half_a, rx_a), rz_a)
+    dt[1] = table_grad(core, 1, dinc)
+    mid_core.wait_recv()
+    mid_z = reduce_slot(1)
+    nt_sib[...] = table_grad(1 - core, 0, sm)
+    rim2_core = remote(nt_sib, nrd, sib)
+    full_b[own_piece] = sum_z(b_z, rz_b)
+    g_bxy, g_bcore = spread(full_b, pl.ds(0, 64))
+    l_z = send_z(sum_xy(l_xy, half_l, rx_l), rz_l)
+    ntd[...] = table_grad(core, 0, sm)
+    rim2_core.wait_recv()
+    ned[...] = (ntd[1 - zl].astype(F32) + nrd[1 - zl].astype(F32)).astype(BF)
+    rim2_z = remote(ned, nre, zpart)
+
+    main_rows, late_rows = pl.ds(0, 80), pl.ds(80, 16)
+    full_a[own_piece, main_rows] = sum_z(a_z, rz_a)
+    g_axy, g_acore = spread(full_a, main_rows)
+    rim2_z.wait_recv()
+    rims2_out[...] = (ntd[zl].astype(F32) + nrd[zl].astype(F32) + nre[...].astype(F32)).astype(BF)
+    to_tails2 = remote(rims2_out.at[low], rims2_in.at[0], below)
+    to_heads2 = remote(rims2_out.at[high], rims2_in.at[1], above)
+    full_a[own_piece, late_rows] = sum_z(l_z, rz_l)
+    g_lxy, g_lcore = spread(full_a, late_rows)
+    forward(g_bxy, g_bcore, full_b, pl.ds(0, 64))
     for c in g_bcore:
         c.wait_recv()
     b_copy = pltpu.make_async_copy(full_b, full_b_out, local_sem.at[8])
     b_copy.start()
-    forward(g_axy, g_acore, full_a)
+    forward(g_axy, g_acore, full_a, main_rows)
+    forward(g_lxy, g_lcore, full_a, late_rows)
 
     mid_z.wait_recv()
-    to_tails.wait_recv()
-    to_heads.wait_recv()
+    for c in (to_tails, to_heads, to_tails2, to_heads2):
+        c.wait_recv()
+    rims2 = jnp.concatenate([rims2_in[1], rims2_in[0]], axis=0)
     dproj = slot_sum(1) + jnp.concatenate([rims_in[1].astype(F32), rims_in[0].astype(F32)], axis=0)
+    dproj = dproj + nn(rims2, wdown2[...])
     coarse = dproj.astype(BF)
     fine = (dproj - coarse.astype(F32)).astype(BF)
     grad[...] = (nt(coarse, wa[...]) + nt(fine, wa[...])).astype(BF)
     grad_copy = pltpu.make_async_copy(grad, grad_out, local_sem.at[6])
     grad_copy.start()
 
-    for c in g_acore:
+    for c in g_acore + g_lcore:
         c.wait_recv()
     a_copy = pltpu.make_async_copy(full_a, full_a_out, local_sem.at[7])
     a_copy.start()
@@ -513,7 +530,7 @@
     Y, ZH, X = dims
     XY, Z = X * Y, 2 * ZH
     nb = 16 // XY
-    transfers = 40 + 7 * (XY - 1) + 5 * (Z - 1)
+    transfers = 48 + 9 * (XY - 1) + 3 * (Z - 1)
     vmem = pl.BlockSpec(memory_space=pltpu.VMEM)
     hbm = pl.BlockSpec(memory_space=pl.ANY)
     index = [a.reshape(16, 128) for a in (edge_src, edge_dst, trip_in, trip_out)]
@@ -539,6 +556,8 @@
             V((2, 2, OWN, WIDTH), BF), V((2, 2, OWN, WIDTH), BF), V((2, 2, OWN, WIDTH), BF),
             V((2, OWN, WIDTH), BF), V((2, OWN, WIDTH), BF), V((OWN, WIDTH), BF),
             V((OWN, WIDTH), BF), V((2, GH, WIDTH), BF),
+            V((2, OWN, 128), BF), V((2, OWN, 128), BF), V((2, OWN, 128), BF),
+            V((OWN, 128), BF), V((OWN, 128), BF), V((OWN, 128), BF), V((2, GH, 128), BF),
             V((512, WIDTH), F32), V((512, WIDTH), F32), V((128, WIDTH), F32), V((128, WIDTH), F32),
             V((128, WIDTH), F32),
             V((SLOTS, WIDTH), BF), V((SLOTS, WIDTH), F32),

time: 94 us -> 98.7 us (1.050)
  Pallas kernels: 91.6 us -> 96.4 us
    pallas_call x1, Pallas kernels: 88 us -> 92.8 us  [per_device(): pl.pallas_call(functools.partial(kernel, dims), out_shape=(jax.ShapeDtype...]
where the time goes in v6:
time: 98.7 us; the launch traced here: 98.5 us
  Pallas kernels  96.4 us (98%)
  between operations  2.1 us (2%)
    pallas_call x1, Pallas kernels, per_device(): pl.pallas_call(functools.partial(kernel, dims), out_shape=(jax.ShapeDtype...  92.8 us
    pallas_call x1, Pallas kernels, per_device(): pl.pallas_call(functools.partial(finish, factor), out_shape=(jax.ShapeDty...  3.6 us

profile of v6, /device:TPU:1, one launch (start us, length us, event | category | flops | bytes accessed | tf_op | source)
XLA Modules:
  0.0 98.5 jit_solution(6130700557180779392)
XLA Ops:
  1.9 92.8 %shard_map.173 = (bf16[32,96,128]{2,1,0:T(8,128)(2,1)}, bf16[32,64,128]{2,1,0:T(8,128)(2,1)}, bf16[256,512]{1,0:T(8,128)(2,1)}) custom-call(s32[1,1]{1,0:T(1,128)} %bitcast.9.ecnt_ref, s32[1,1]{1,0:T(1,128)} %bitcast.10.tcnt_ref, s32[16,128]{1,0:T(8,128)} %bitcast.14, s32[16,128]{1,0:T(8,128)} %bitcast.15, s32[16,128]{1,0:T(8,128)} %bitcast.16, ...), custom_call_target="tpu_custom_call" | custom-call | tf_op jit(solution)/shard_map/pallas_call | solution.py:539
  94.8 3.6 %shard_map.174 = (bf16[256,512]{1,0:T(8,128)(2,1)}, f32[512,512]{1,0:T(8,128)}, f32[64,512]{1,0:T(8,128)}, f32[64,512]{1,0:T(8,128)}, f32[512,512]{1,0:T(8,128)}) custom-call(bf16[256,512]{1,0:T(8,128)(2,1)} %get-tuple-element.13.grad_hbm, bf16[32,96,128]{2,1,0:T(8,128)(2,1)} %get-tuple-element.14.full_a_hbm, ...), custom_call_target="tpu_custom_call" | custom-call | tf_op jit(solution)/shard_map/pallas_call | solution.py:581

commit v7 on v5

--- a/solution.py
+++ b/solution.py
@@ -184,10 +184,7 @@
         return pl.ds(pl.multiple_of(b * BLK, BLK), BLK)
 
     def gather(index, first, source):
-        got = nn(pick_columns(index, first, OWN), source[0])
-        for k in range(1, 4):
-            got = got + nn(pick_columns(index, first + k * OWN, OWN), source[k])
-        return got
+        return nn(pick_columns(index, first, 4 * OWN), source[...].reshape(4 * OWN, WIDTH))
 
     def edge_own(b, carry):
         picked[block(b)] = gather(src_col[block(b)], 0, mid).astype(BF)
@@ -386,16 +383,11 @@
 
     def table_grad(owner, part, out):
         first = (4 + owner) * OWN if part == 0 else owner * OWN
-        total = None
-        for b in range(SLOTS // BLK):
-            cols = slice(BLK * b, BLK * (b + 1))
-            line = rows[0:1, cols]
-            choice = jnp.concatenate(
-                [pick_rows(line, first, OWN), pick_rows(line, first + 2 * OWN, OWN)], axis=0
-            )
-            term = nn(choice, dinc[cols])
-            total = term if total is None else total + term
-        total = total.astype(BF)
+        line = rows[0:1, :]
+        choice = jnp.concatenate(
+            [pick_rows(line, first, OWN), pick_rows(line, first + 2 * OWN, OWN)], axis=0
+        )
+        total = nn(choice, dinc[...]).astype(BF)
         out[part, 0] = total[0:OWN]
         out[part, 1] = total[OWN:]
 
@@ -437,6 +429,8 @@
     b_copy = pltpu.make_async_copy(full_b, full_b_out, local_sem.at[8])
     b_copy.start()
     forward(g_axy, g_acore, full_a)
+    own_copy = pltpu.make_async_copy(full_a.at[mine], full_a_out.at[mine], local_sem.at[9])
+    own_copy.start()
 
     mid_z.wait_recv()
     to_tails.wait_recv()
@@ -450,13 +444,14 @@
 
     for c in g_acore:
         c.wait_recv()
-    a_copy = pltpu.make_async_copy(full_a, full_a_out, local_sem.at[7])
+    a_copy = pltpu.make_async_copy(full_a.at[not_mine], full_a_out.at[not_mine], local_sem.at[7])
     a_copy.start()
     for c in started:
         c.wait_send()
     b_copy.wait()
     grad_copy.wait()
     a_copy.wait()
+    own_copy.wait()
 
 
 def finish(
@@ -549,7 +544,7 @@
             V((32, 16, 128), BF), V((16, 16, 128), BF), V((16, 16, 128), BF), V((XY - 1, nb, 16, 128), BF),
             V((Z, nb, 16, 128), BF),
             pltpu.SemaphoreType.DMA((transfers,)), pltpu.SemaphoreType.DMA((transfers,)),
-            pltpu.SemaphoreType.DMA((9,)),
+            pltpu.SemaphoreType.DMA((10,)),
         ],
         compiler_params=pltpu.CompilerParams(
             collective_id=0, has_side_effects=True, vmem_limit_bytes=60 * 1024 * 1024

time: 94 us -> 93.8 us (level)
  no operation moved by 1% of the time
where the time goes in v7:
time: 93.8 us; the launch traced here: 93.6 us
  Pallas kernels  91.5 us (98%)
  between operations  2.1 us (2%)
    pallas_call x1, Pallas kernels, per_device(): pl.pallas_call(functools.partial(kernel, dims), out_shape=(jax.ShapeDtype...  87.9 us
    pallas_call x1, Pallas kernels, per_device(): pl.pallas_call(functools.partial(finish, factor), out_shape=(jax.ShapeDty...  3.61 us

profile of v7, /device:TPU:1, one launch (start us, length us, event | category | flops | bytes accessed | tf_op | source)
XLA Modules:
  0.0 93.6 jit_solution(8261276365779155381)
XLA Ops:
  1.9 87.9 %shard_map.173 = (bf16[32,96,128]{2,1,0:T(8,128)(2,1)}, bf16[32,64,128]{2,1,0:T(8,128)(2,1)}, bf16[256,512]{1,0:T(8,128)(2,1)}) custom-call(s32[1,1]{1,0:T(1,128)} %bitcast.9.ecnt_ref, s32[1,1]{1,0:T(1,128)} %bitcast.10.tcnt_ref, s32[16,128]{1,0:T(8,128)} %bitcast.14, s32[16,128]{1,0:T(8,128)} %bitcast.15, s32[16,128]{1,0:T(8,128)} %bitcast.16, ...), custom_call_target="tpu_custom_call" | custom-call | tf_op jit(solution)/shard_map/pallas_call | solution.py:517
  89.8 3.6 %shard_map.174 = (bf16[256,512]{1,0:T(8,128)(2,1)}, f32[512,512]{1,0:T(8,128)}, f32[64,512]{1,0:T(8,128)}, f32[64,512]{1,0:T(8,128)}, f32[512,512]{1,0:T(8,128)}) custom-call(bf16[256,512]{1,0:T(8,128)(2,1)} %get-tuple-element.13.grad_hbm, bf16[32,96,128]{2,1,0:T(8,128)(2,1)} %get-tuple-element.14.full_a_hbm, ...), custom_call_target="tpu_custom_call" | custom-call | tf_op jit(solution)/shard_map/pallas_call | solution.py:557
